TPU v7x, 32 devices: a whole 2x2x4 slice. The times are simulated.
32 devices in a mesh: fsdp: 16 (over z, x, core), seq: 2 (over y).
Axes of the slice: x: 2, y: 2, z: 4, core: 2. Of those that a mesh axis runs over, the one named last changes fastest.
Arguments:
- tokens: bfloat16 [16, 1024, 1024], P('fsdp', 'seq'), may hold values from -6 to 6
- positions: int32 [3, 16, 1024], P(None, 'fsdp', 'seq'), may hold values from 0 to 15
- ln1_gain: bfloat16 [1024], P('fsdp'), may hold values from 0.099609375 to 1.8984375
- ln1_bias: bfloat16 [1024], P('fsdp'), may hold values from -3 to 3
- qkv_weight: bfloat16 [1024, 3072], P('fsdp'), may hold values from -0.1875 to 0.1875
- qkv_bias: bfloat16 [3072], P('fsdp'), may hold values from -0.19921875 to 0.19921875
- out_weight: bfloat16 [1024, 1024], P('fsdp'), may hold values from -4 to 4
- out_bias: bfloat16 [1024], P('fsdp'), may hold values from -3 to 3
- ln2_gain: bfloat16 [1024], P('fsdp'), may hold values from 0.099609375 to 1.8984375
- ln2_bias: bfloat16 [1024], P('fsdp'), may hold values from -3 to 3
- fc1_weight: bfloat16 [1024, 4096], P('fsdp'), may hold values from -0.1875 to 0.1875
- fc1_bias: bfloat16 [4096], P('fsdp'), may hold values from -3 to 3
- fc2_weight: bfloat16 [4096, 1024], P('fsdp'), may hold values from -0.09375 to 0.09375
- fc2_bias: bfloat16 [1024], P('fsdp'), may hold values from -3 to 3
- out_grad: bfloat16 [16, 1024, 1024], P('fsdp', 'seq'), may hold values from -6 to 6
Outputs:
- block_out: bfloat16 [16, 1024, 1024], P('fsdp', 'seq')
- tokens_grad: float32 [16, 1024, 1024], P('fsdp', 'seq')
- ln1_gain_grad: float32 [1024], P('fsdp')
- ln1_bias_grad: float32 [1024], P('fsdp')
- qkv_weight_grad: float32 [1024, 3072], P('fsdp')
- qkv_bias_grad: float32 [3072], P('fsdp')
- out_weight_grad: float32 [1024, 1024], P('fsdp')
- out_bias_grad: float32 [1024], P('fsdp')
- ln2_gain_grad: float32 [1024], P('fsdp')
- ln2_bias_grad: float32 [1024], P('fsdp')
- fc1_weight_grad: float32 [1024, 4096], P('fsdp')
- fc1_bias_grad: float32 [4096], P('fsdp')
- fc2_weight_grad: float32 [4096, 1024], P('fsdp')
- fc2_bias_grad: float32 [1024], P('fsdp')
All inputs are finite; a program needn't handle non-finite values.
Results may differ from a plain program's by a relative error of at most 0.011.
Values may be sent and summed in bfloat16 or wider, within the bound.
No kernel may reach another device: no remote copies, remote signals or barrier semaphores. Data moves between devices by JAX's collectives and lax.ppermute only.
A program may use at most 192 MiB of HBM per device.

v0:
```python
import jax
import jax.numpy as jnp
from jax import lax
from jax.sharding import PartitionSpec as P

D = 1024
HEADS = 16
HD = 64


eps_norm = 1e-06
theta_base = 10000.0


def layer_norm(values, gain, shift):
    center = values - jnp.mean(values, axis=-1, keepdims=True)
    spread = jnp.mean(center * center, axis=-1, keepdims=True)
    return center * lax.rsqrt(spread + eps_norm) * gain + shift


def gelu_exact(values):
    return 0.5 * values * (1.0 + lax.erf(values * 0.7071067811865476))


def rotary_tables(index_rows, head_dim):
    rot_width = 2 * (head_dim // 3 // 2)
    half_width = rot_width // 2
    exponent = jnp.arange(half_width).astype(jnp.float32) * (2.0 / rot_width)
    freqs = jnp.power(jnp.float32(theta_base), -exponent)
    angles = index_rows.astype(jnp.float32)[:, :, None] * freqs
    return (jnp.cos(angles), jnp.sin(angles))


def rotate(values, cosines, sines):
    half_width = cosines.shape[-1]
    rot_width = 2 * half_width
    pieces = []
    for axis_number in range(3):
        offset = axis_number * rot_width
        leading = values[:, :, offset : offset + half_width]
        trailing = values[:, :, offset + half_width : offset + rot_width]
        cosine_part = cosines[axis_number][:, None, :]
        sine_part = sines[axis_number][:, None, :]
        pieces.append(leading * cosine_part - trailing * sine_part)
        pieces.append(trailing * cosine_part + leading * sine_part)
    pieces.append(values[:, :, 3 * rot_width :])
    return jnp.concatenate(pieces, axis=-1)


def attend_forward(query_heads, key_heads, value_heads):
    length, columns = query_heads.shape
    head_count = columns // HD
    block = min(512, length)
    count = length // block
    scale = HD ** (-0.5)
    keys = key_heads.reshape(length, head_count, HD)
    values_all = value_heads.reshape(length, head_count, HD)

    def one_block(query_block):
        query_block = query_block.reshape(block, head_count, HD)
        scores = (
            jnp.einsum("qhd,khd->hqk", query_block, keys, preferred_element_type=jnp.float32)
            * scale
        )
        peak = jnp.max(scores, axis=-1, keepdims=True)
        weights = jnp.exp(scores - peak)
        totals = jnp.sum(weights, axis=-1, keepdims=True)
        probs_low = (weights / totals).astype(jnp.bfloat16)
        result = jnp.einsum(
            "hqk,khd->qhd", probs_low, values_all, preferred_element_type=jnp.float32
        )
        return (result.reshape(block, columns), (peak + jnp.log(totals))[:, :, 0])

    results, log_totals = lax.map(one_block, query_heads.reshape(count, block, columns))
    return (results.reshape(length, columns), log_totals)


def attend_backward(query_heads, key_heads, value_heads, log_totals, grad_heads):
    length, columns = query_heads.shape
    head_count = columns // HD
    block = min(512, length)
    count = length // block
    scale = HD ** (-0.5)
    keys = key_heads.reshape(length, head_count, HD)
    values_all = value_heads.reshape(length, head_count, HD)

    def one_block(carry, inputs):
        key_total, value_total = carry
        query_block, grad_block, log_block = inputs
        query_block = query_block.reshape(block, head_count, HD)
        grad_block = grad_block.reshape(block, head_count, HD)
        scores = (
            jnp.einsum("qhd,khd->hqk", query_block, keys, preferred_element_type=jnp.float32)
            * scale
        )
        probs = jnp.exp(scores - log_block[:, :, None])
        probs_low = probs.astype(jnp.bfloat16)
        prob_grad = jnp.einsum(
            "qhd,khd->hqk", grad_block, values_all, preferred_element_type=jnp.float32
        )
        inner = jnp.sum(probs * prob_grad, axis=-1, keepdims=True)
        score_grad = (probs * (prob_grad - inner)).astype(jnp.bfloat16)
        query_grad = (
            jnp.einsum("hqk,khd->qhd", score_grad, keys, preferred_element_type=jnp.float32) * scale
        )
        key_total = (
            key_total
            + jnp.einsum(
                "hqk,qhd->khd", score_grad, query_block, preferred_element_type=jnp.float32
            )
            * scale
        )
        value_total = value_total + jnp.einsum(
            "hqk,qhd->khd", probs_low, grad_block, preferred_element_type=jnp.float32
        )
        return ((key_total, value_total), query_grad.reshape(block, columns).astype(jnp.bfloat16))

    empty = jnp.zeros((length, head_count, HD), jnp.float32)
    inputs = (
        query_heads.reshape(count, block, columns),
        grad_heads.reshape(count, block, columns),
        log_totals,
    )
    (key_total, value_total), query_grads = lax.scan(one_block, (empty, empty), inputs)
    return (
        query_grads.reshape(length, columns),
        key_total.reshape(length, columns).astype(jnp.bfloat16),
        value_total.reshape(length, columns).astype(jnp.bfloat16),
    )


def on_device(
    tokens,
    positions,
    ln1_gain,
    ln1_bias,
    qkv_weight,
    qkv_bias,
    out_weight,
    out_bias,
    ln2_gain,
    ln2_bias,
    fc1_weight,
    fc1_bias,
    fc2_weight,
    fc2_bias,
    out_grad,
):
    gathered = (
        lax.all_gather(ln1_gain, "fsdp", axis=0, tiled=True),
        lax.all_gather(ln1_bias, "fsdp", axis=0, tiled=True),
        lax.all_gather(qkv_weight, "fsdp", axis=0, tiled=True),
        lax.all_gather(qkv_bias, "fsdp", axis=0, tiled=True),
        lax.all_gather(out_weight, "fsdp", axis=0, tiled=True),
        lax.all_gather(out_bias, "fsdp", axis=0, tiled=True),
        lax.all_gather(ln2_gain, "fsdp", axis=0, tiled=True),
        lax.all_gather(ln2_bias, "fsdp", axis=0, tiled=True),
        lax.all_gather(fc1_weight, "fsdp", axis=0, tiled=True),
        lax.all_gather(fc1_bias, "fsdp", axis=0, tiled=True),
        lax.all_gather(fc2_weight, "fsdp", axis=0, tiled=True),
        lax.all_gather(fc2_bias, "fsdp", axis=0, tiled=True),
    )
    (
        gain_one,
        bias_one,
        w_qkv,
        b_qkv,
        w_out,
        b_out,
        gain_two,
        bias_two,
        w_up,
        b_up,
        w_down,
        b_down,
    ) = gathered
    rows = tokens.shape[1]
    tokens_f = tokens[0].astype(jnp.float32)
    cosines, sines = rotary_tables(positions[:, 0, :], HD)
    normed_one, norm_one_back = jax.vjp(
        layer_norm, tokens_f, gain_one.astype(jnp.float32), bias_one.astype(jnp.float32)
    )
    normed_one_low = normed_one.astype(jnp.bfloat16)
    mixed = jnp.dot(normed_one_low, w_qkv, preferred_element_type=jnp.float32) + b_qkv.astype(
        jnp.float32
    )
    queries = (
        rotate(mixed[:, :D].reshape(rows, HEADS, HD), cosines, sines)
        .reshape(rows, D)
        .astype(jnp.bfloat16)
    )
    keys_tok = (
        rotate(mixed[:, D : 2 * D].reshape(rows, HEADS, HD), cosines, sines)
        .reshape(rows, D)
        .astype(jnp.bfloat16)
    )
    values_tok = mixed[:, 2 * D :].astype(jnp.bfloat16)
    query_heads, key_heads, value_heads = (
        lax.all_to_all(queries, "seq", split_axis=1, concat_axis=0, tiled=True),
        lax.all_to_all(keys_tok, "seq", split_axis=1, concat_axis=0, tiled=True),
        lax.all_to_all(values_tok, "seq", split_axis=1, concat_axis=0, tiled=True),
    )
    attended, log_totals = attend_forward(query_heads, key_heads, value_heads)
    attended_tok = lax.all_to_all(
        attended.astype(jnp.bfloat16), "seq", split_axis=0, concat_axis=1, tiled=True
    )
    hidden = (
        tokens_f
        + jnp.dot(attended_tok, w_out, preferred_element_type=jnp.float32)
        + b_out.astype(jnp.float32)
    )
    normed_two, norm_two_back = jax.vjp(
        layer_norm, hidden, gain_two.astype(jnp.float32), bias_two.astype(jnp.float32)
    )
    normed_two_low = normed_two.astype(jnp.bfloat16)
    preact = jnp.dot(normed_two_low, w_up, preferred_element_type=jnp.float32) + b_up.astype(
        jnp.float32
    )
    activated, gelu_back = jax.vjp(gelu_exact, preact)
    act_low = activated.astype(jnp.bfloat16)
    result = (
        hidden
        + jnp.dot(act_low, w_down, preferred_element_type=jnp.float32)
        + b_down.astype(jnp.float32)
    )
    block_out = result.astype(jnp.bfloat16)[None]
    w_qkv, w_out, w_up, w_down = (
        lax.all_gather(qkv_weight, "fsdp", axis=0, tiled=True),
        lax.all_gather(out_weight, "fsdp", axis=0, tiled=True),
        lax.all_gather(fc1_weight, "fsdp", axis=0, tiled=True),
        lax.all_gather(fc2_weight, "fsdp", axis=0, tiled=True),
    )
    cotangent = out_grad[0]
    cotangent_f = cotangent.astype(jnp.float32)
    down_grad = jnp.einsum("tf,td->fd", act_low, cotangent, preferred_element_type=jnp.float32)
    down_bias_grad = jnp.sum(cotangent_f, axis=0)
    act_grad = jnp.einsum("td,fd->tf", cotangent, w_down, preferred_element_type=jnp.float32)
    pre_grad = gelu_back(act_grad)[0].astype(jnp.bfloat16)
    up_grad = jnp.einsum("td,tf->df", normed_two_low, pre_grad, preferred_element_type=jnp.float32)
    up_bias_grad = jnp.sum(pre_grad.astype(jnp.float32), axis=0)
    normed_two_grad = jnp.einsum("tf,df->td", pre_grad, w_up, preferred_element_type=jnp.float32)
    hidden_part, gain_two_grad, bias_two_grad = norm_two_back(normed_two_grad)
    hidden_grad = cotangent_f + hidden_part
    branch_low = hidden_grad.astype(jnp.bfloat16)
    out_w_grad = jnp.einsum(
        "te,td->ed", attended_tok, branch_low, preferred_element_type=jnp.float32
    )
    out_b_grad = jnp.sum(branch_low.astype(jnp.float32), axis=0)
    attended_grad = jnp.einsum(
        "td,ed->te", branch_low, w_out, preferred_element_type=jnp.float32
    ).astype(jnp.bfloat16)
    grad_heads = lax.all_to_all(attended_grad, "seq", split_axis=1, concat_axis=0, tiled=True)
    query_grad, key_grad, value_grad = attend_backward(
        query_heads, key_heads, value_heads, log_totals, grad_heads
    )
    query_tok, key_tok, value_tok = (
        lax.all_to_all(query_grad, "seq", split_axis=0, concat_axis=1, tiled=True),
        lax.all_to_all(key_grad, "seq", split_axis=0, concat_axis=1, tiled=True),
        lax.all_to_all(value_grad, "seq", split_axis=0, concat_axis=1, tiled=True),
    )
    query_back = (
        rotate(query_tok.astype(jnp.float32).reshape(rows, HEADS, HD), cosines, -sines)
        .reshape(rows, D)
        .astype(jnp.bfloat16)
    )
    key_back = (
        rotate(key_tok.astype(jnp.float32).reshape(rows, HEADS, HD), cosines, -sines)
        .reshape(rows, D)
        .astype(jnp.bfloat16)
    )
    qkv_grad = jnp.concatenate([query_back, key_back, value_tok], axis=1)
    qkv_w_grad = jnp.einsum(
        "td,tc->dc", normed_one_low, qkv_grad, preferred_element_type=jnp.float32
    )
    qkv_b_grad = jnp.sum(qkv_grad.astype(jnp.float32), axis=0)
    normed_one_grad = jnp.einsum("tc,dc->td", qkv_grad, w_qkv, preferred_element_type=jnp.float32)
    token_part, gain_one_grad, bias_one_grad = norm_one_back(normed_one_grad)
    tokens_grad = (hidden_grad + token_part)[None]
    owned = (
        lax.psum_scatter(gain_one_grad, "fsdp", scatter_dimension=0, tiled=True),
        lax.psum_scatter(bias_one_grad, "fsdp", scatter_dimension=0, tiled=True),
        lax.psum_scatter(qkv_w_grad, "fsdp", scatter_dimension=0, tiled=True),
        lax.psum_scatter(qkv_b_grad, "fsdp", scatter_dimension=0, tiled=True),
        lax.psum_scatter(out_w_grad, "fsdp", scatter_dimension=0, tiled=True),
        lax.psum_scatter(out_b_grad, "fsdp", scatter_dimension=0, tiled=True),
        lax.psum_scatter(gain_two_grad, "fsdp", scatter_dimension=0, tiled=True),
        lax.psum_scatter(bias_two_grad, "fsdp", scatter_dimension=0, tiled=True),
        lax.psum_scatter(up_grad, "fsdp", scatter_dimension=0, tiled=True),
        lax.psum_scatter(up_bias_grad, "fsdp", scatter_dimension=0, tiled=True),
        lax.psum_scatter(down_grad, "fsdp", scatter_dimension=0, tiled=True),
        lax.psum_scatter(down_bias_grad, "fsdp", scatter_dimension=0, tiled=True),
    )
    own_a, own_b, own_c, own_d, own_e, own_f, own_g, own_h, own_i, own_j, own_k, own_l = owned
    summed = lax.psum(
        (own_a, own_b, own_c, own_d, own_e, own_f, own_g, own_h, own_i, own_j, own_k, own_l), "seq"
    )
    return (
        block_out,
        tokens_grad,
        summed[0],
        summed[1],
        summed[2],
        summed[3],
        summed[4],
        summed[5],
        summed[6],
        summed[7],
        summed[8],
        summed[9],
        summed[10],
        summed[11],
    )


def solution(mesh):
    return jax.shard_map(
        on_device,
        mesh=mesh,
        in_specs=(
            P("fsdp", "seq", None),
            P(None, "fsdp", "seq"),
            P("fsdp"),
            P("fsdp"),
            P("fsdp", None),
            P("fsdp"),
            P("fsdp", None),
            P("fsdp"),
            P("fsdp"),
            P("fsdp"),
            P("fsdp", None),
            P("fsdp"),
            P("fsdp", None),
            P("fsdp"),
            P("fsdp", "seq", None),
        ),
        out_specs=(
            P("fsdp", "seq", None),
            P("fsdp", "seq", None),
            P("fsdp"),
            P("fsdp"),
            P("fsdp", None),
            P("fsdp"),
            P("fsdp", None),
            P("fsdp"),
            P("fsdp"),
            P("fsdp"),
            P("fsdp", None),
            P("fsdp"),
            P("fsdp", None),
            P("fsdp"),
        ),
        check_vma=False,
    )
```

profile of v0, /device:TPU:0, one launch (start us, length us, event | category | flops | bytes accessed | tf_op | source)
XLA Modules:
  0.0 1087.5 jit_solution(4961339951127485053)
XLA Ops:
  16.9 64.2 %all-reduce.18 = (bf16[3072]{0:T(1024)(128)(2,1)S(1)}, bf16[1024]{0:T(1024)(128)(2,1)S(1)}, bf16[1024]{0:T(1024)(128)(2,1)S(1)}, bf16[1024]{0:T(1024)(128)(2,1)}...) all-reduce(bf16[3072]{0:T(1024)(128)(2,1)S(1)} %dynamic-update-slic, ...), channel_id=1, replica_groups=mesh['fsdp'=16,'seq'=2] {'fsdp'}, use_global_device_ids=true, to_apply=%add.2 | all-reduce | flops 9216 | bytes 36864
  82.8 5.9 convolution_add_fusion
  88.8 2.7 copy-done.8
  92.6 3.6 all-to-all-start.2
  96.2 4.9 fusion.47
  103.7 2.3 add_convert_fusion.9
  106.0 20.7 %concatenate.20 = bf16[512,16,64]{0,2,1:T(8,128)(2,1)} concatenate(bf16[512,16,10]{0,2,1:T(8,128)(2,1)} %get-tuple-element.256, bf16[512,16,10]{0,2,1:T(8,128)(2,1)} %get-tuple-element.257, bf16[512,16,10]{0,2,1:T(8,128)(2,1)} %get-tuple-element.254, bf16[512,16,10]{0,2,1:T(8,128)(2,1)} %get-tuple-element.255, bf16[512,16,10]{0,2,1:T(8,128)(2,1)} %get-tuple-element.235, ...), dimensions={2} | concatenate | bytes 2097152 | tf_op jit(solution)/shard_map/concatenate | solution.py:47
  126.8 4.4 all-to-all-start.1
  133.8 2.4 add_convert_fusion.12
  136.2 20.8 %concatenate.19 = bf16[512,16,64]{0,2,1:T(8,128)(2,1)} concatenate(bf16[512,16,10]{0,2,1:T(8,128)(2,1)} %get-tuple-element.260, bf16[512,16,10]{0,2,1:T(8,128)(2,1)} %get-tuple-element.261, bf16[512,16,10]{0,2,1:T(8,128)(2,1)} %get-tuple-element.258, bf16[512,16,10]{0,2,1:T(8,128)(2,1)} %get-tuple-element.259, bf16[512,16,10]{0,2,1:T(8,128)(2,1)} %get-tuple-element.241, ...), dimensions={2} | concatenate | bytes 2097152 | tf_op jit(solution)/shard_map/concatenate | solution.py:47
  156.9 4.6 all-to-all-start
  164.2 2.3 copy.58
  167.2 4.0 all-to-all-done
  171.2 27.6 %while.27 = (s32[]{:T(128)}, bf16[2,512,512]{1,2,0:T(8,128)(2,1)}, f32[2,8,512]{2,1,0:T(8,128)}, bf16[2,512,512]{1,2,0:T(8,128)(2,1)}, bf16[1024,8,64]{0,2,1:T(8...) while((s32[]{:T(128)}, bf16[2,512,512]{1,2,0:T(8,128)(2,1)}, f32[2,8,512]{2,1,0:T(8,128)}, ...), condition=%wide.region_5.6_spmd, body=%wide.region_2.5_spmd.sunk | while | flops 1111486464 | bytes 64094360 | solution.py:74
  172.4 2.5 multiply_reduce_fusion.7
  174.9 3.4 fusion.100
  178.4 5.0 fusion.101
  186.2 2.5 multiply_reduce_fusion.7
  188.7 3.4 fusion.100
  192.1 5.1 fusion.101
  198.9 4.5 all-to-all-start.3
  203.4 18.8 %all-gather = bf16[16,1,256]{2,1,0:T(2,128)(2,1)S(1)} all-gather(bf16[1,1,256]{2,1,0:T(2,128)(2,1)S(1)} %reshape.268), channel_id=1, replica_groups=mesh['fsdp'=16,'seq'=2] {'fsdp'}, dimensions={0}, use_global_device_ids=true | all-gather | bytes 8704 | tf_op jit(solution)/shard_map/all_gather | solution.py:159
  222.3 4.5 fusion.49
  229.1 11.3 %multiply_convert_fusion.1 = (bf16[512,4096]{1,0:T(8,128)(2,1)}, f32[512,4096]{1,0:T(8,128)}) fusion(f32[4096]{0:T(1024)S(1)} %bitcast.230, bf16[1024,4096]{1,0:T(8,128)(2,1)} %all-gather.10.cloned.1.call-done, f32[512,1024]{1,0:T(8,128)} %get-tuple-element.279, f32[1024]{0:T(1024)S(1)} %convert_element_type.176, f32[1024]{0:T(1024)S(1)} %convert_element_type.175, ...), kind=kOutput, calls=%fused_computation.27 | convolution fusion | flops 4310171648 | bytes 23097344 | tf_op jit(solution)/shard_map/dot_general | solution.py:216
  240.4 28.7 %all-gather.12.cloned.1.call-done = bf16[4096,1024]{1,0:T(8,128)(2,1)} async-done(((bf16[256,1024]{1,0:T(8,128)(2,1)}), bf16[4096,1024]{1,0:T(8,128)(2,1)}) %all-gather.12.cloned.1.call-update) | async-done | bytes 8388624 | tf_op jit(solution)/shard_map/all_gather | solution.py:160
  269.2 12.6 %convert_reduce_fusion = (f32[4096]{0:T(1024)}, bf16[512,4096]{1,0:T(8,128)(2,1)S(1)}) fusion(bf16[4096,1024]{1,0:T(8,128)(2,1)} %all-gather.12.cloned.1.call-done, bf16[1,512,1024]{2,1,0:T(8,128)(2,1)S(1)} %copy-done.9, f32[512,4096]{1,0:T(8,128)} %get-tuple-element.281, f32[4096]{0:T(1024)S(1)} %bitcast.231), kind=kOutput, calls=%fused_computation.25 | convolution fusion | flops 4328517632 | bytes 22052864 | tf_op jit(solution)/shard_map/td,fd->tf/dot_general | solution.py:237
  281.8 8.7 multiply_reduce_fusion.2
  290.6 2.3 fusion.46
  298.5 2.4 copy.64
  300.8 4.4 all-to-all-start.4
  305.4 4.5 fusion.51
  309.9 9.8 all-to-all-done.4
  319.7 81.4 %while.28 = (s32[]{:T(128)}, f32[1024,8,64]{0,2,1:T(8,128)}, f32[1024,8,64]{0,2,1:T(8,128)}, bf16[2,512,512]{1,2,0:T(8,128)(2,1)}, bf16[2,512,512]{1,2,0:T(8,128...) while((s32[]{:T(128)}, f32[1024,8,64]{0,2,1:T(8,128)}, ...), condition=%wide.region_12.13_spmd.clone, body=%wide.region_10.12_spmd.clone.sunk | while | flops 2737827840 | bytes 185188592 | solution.py:124
  321.9 2.4 fusion.112
  324.3 4.4 bitcast_add_fusion.5
  328.7 9.8 multiply_reduce_fusion.8
  338.5 10.5 multiply_convert_fusion.3
  349.0 6.2 fusion.113
  355.2 2.9 bitcast_add_fusion.4
  361.1 2.4 fusion.112
  363.5 5.6 bitcast_add_fusion.5
  369.1 9.7 multiply_reduce_fusion.8
  378.8 10.4 multiply_convert_fusion.3
  389.2 6.2 fusion.113
  395.5 4.6 bitcast_add_fusion.4
  401.1 3.7 all-to-all-start.5
  408.9 9.6 all-to-all-done.5
  418.5 3.6 all-to-all-start.6
  426.1 2.4 copy.63
  430.7 4.3 all-to-all-done.6
  434.9 4.4 all-to-all-start.7
  443.5 18.7 %concatenate.21 = bf16[512,16,64]{0,2,1:T(8,128)(2,1)} concatenate(bf16[512,16,10]{0,2,1:T(8,128)(2,1)S(1)} %get-tuple-element.248, bf16[512,16,10]{0,2,1:T(8,128)(2,1)} %get-tuple-element.249, bf16[512,16,10]{0,2,1:T(8,128)(2,1)S(1)} %get-tuple-element.246, bf16[512,16,10]{0,2,1:T(8,128)(2,1)S(1)} %get-tuple-element.247, bf16[512,16,10]{0,2,1:T(8,128)(2,1)S(1)} %get-tuple-element.223, ...), dimensions={2} | concatenate | bytes 2097152 | tf_op jit(solution)/shard_map/concatenate | solution.py:47
  462.2 2.4 add_convert_fusion.3
  464.6 12.4 %concatenate.22 = bf16[512,16,64]{0,2,1:T(8,128)(2,1)S(1)} concatenate(bf16[512,16,10]{0,2,1:T(8,128)(2,1)} %get-tuple-element.252, bf16[512,16,10]{0,2,1:T(8,128)(2,1)} %get-tuple-element.253, bf16[512,16,10]{0,2,1:T(8,128)(2,1)} %get-tuple-element.250, bf16[512,16,10]{0,2,1:T(8,128)(2,1)} %get-tuple-element.251, bf16[512,16,10]{0,2,1:T(8,128)(2,1)} %get-tuple-element.229, ...), dimensions={2} | concatenate | bytes 2097152 | tf_op jit(solution)/shard_map/concatenate | solution.py:47
  477.1 9.9 fusion.37
  487.6 15.7 %fusion.42 = f32[1024,4096]{1,0:T(8,128)} fusion(bf16[512,4096]{1,0:T(8,128)(2,1)} %copy-done.65, f32[512,1024]{1,0:T(8,128)} %get-tuple-element.279, f32[1024]{0:T(1024)S(1)} %copy-done.49, f32[1024]{0:T(1024)S(1)} %copy-done.42, f32[512]{0:T(512)S(1)} %copy-done.44, f32[512]{0:T(512)S(1)} %copy-done.38), kind=kOutput, calls=%fused_computation.121 | convolution fusion | flops 4297588736 | bytes 23080960 | tf_op jit(solution)/shard_map/td,tf->df/dot_general | solution.py:239
  504.7 11.0 %fusion.28 = f32[4096,1024]{1,0:T(8,128)} fusion(bf16[512,4096]{1,0:T(8,128)(2,1)} %get-tuple-element.280, bf16[1,512,1024]{2,1,0:T(8,128)(2,1)S(1)} %copy-done.10), kind=kOutput, calls=%fused_computation.64 | convolution fusion | flops 4294967296 | bytes 22020096 | tf_op jit(solution)/shard_map/tf,td->fd/dot_general | solution.py:235
  517.7 102.2 %reduce-scatter.5.cloned.1.call-done = f32[64,3072]{1,0:T(8,128)} async-done(((f32[1024,3072]{1,0:T(8,128)}), f32[64,3072]{1,0:T(8,128)}) %reduce-scatter.5.cloned.1.call-update) | async-done | bytes 786448 | tf_op jit(solution)/shard_map/reduce_scatter | solution.py:282
  619.9 182.4 %reduce-scatter.9.cloned.1.call-done = f32[64,4096]{1,0:T(8,128)} async-done(((f32[1024,4096]{1,0:T(8,128)}), f32[64,4096]{1,0:T(8,128)}) %reduce-scatter.9.cloned.1.call-update) | async-done | bytes 1048592 | tf_op jit(solution)/shard_map/reduce_scatter | solution.py:288
  802.3 182.3 %reduce-scatter.11.cloned.1.call-done = f32[256,1024]{1,0:T(8,128)} async-done(((f32[4096,1024]{1,0:T(8,128)}), f32[256,1024]{1,0:T(8,128)}) %reduce-scatter.11.cloned.1.call-update) | async-done | bytes 1048592 | tf_op jit(solution)/shard_map/reduce_scatter | solution.py:290
  984.6 10.7 fusion.26
  995.3 7.0 fusion.44
  1007.7 59.6 %all-reduce.15 = (f32[1024]{0:T(1024)S(1)}, f32[1024]{0:T(1024)S(1)}, f32[3072]{0:T(1024)S(1)}, f32[1024]{0:T(1024)S(1)}, f32[1024]{0:T(1024)S(1)}, /*index=5*/f...) all-reduce(f32[1024]{0:T(1024)S(1)} %get-tuple-element.148, ...), channel_id=2, replica_groups=mesh['fsdp'=16,'seq'=2] {'fsdp'}, use_global_device_ids=true, to_apply=%region_16.17.clone | all-reduce | flops 13312 | bytes 106496
  1067.9 5.5 all-reduce.16
  (262 shorter events, 68.8 us)
Async XLA Ops:
  7.2 7.0 copy-start.2
  7.2 8.0 copy-start.45
  7.2 8.0 copy-start.57
  7.2 8.2 copy-start.58
  7.2 8.5 copy-start.59
  7.2 8.7 copy-start.60
  7.2 8.9 copy-start.61
  7.3 9.1 copy-start.62
  7.3 9.4 copy-start.63
  7.3 75.5 %all-gather.6.cloned.1.call-start = ((), (), s32[]{:S(2)}) async-start(), calls=%async_computation.12 | async-start | bytes 6684672 | tf_op jit(solution)/shard_map/all_gather | solution.py:152
  8.0 214.2 %all-gather.8.cloned.1.call-start = ((), (), s32[]{:S(2)}) async-start(), calls=%async_computation.13 | async-start | bytes 2228224 | tf_op jit(solution)/shard_map/all_gather | solution.py:154
  8.8 220.3 %all-gather.10.cloned.1.call-start = ((), (), s32[]{:S(2)}) async-start(), calls=%async_computation.14 | async-start | bytes 8912896 | tf_op jit(solution)/shard_map/all_gather | solution.py:158
  9.5 259.7 %all-gather.12.cloned.1.call-start = ((), (), s32[]{:S(2)}) async-start(), calls=%async_computation.15 | async-start | bytes 8912896 | tf_op jit(solution)/shard_map/all_gather | solution.py:160
  14.1 74.6 %copy-start.29 = (f32[512]{0:T(512)}, f32[512]{0:T(512)S(1)}, u32[]{:S(2)}) copy-start(f32[512]{0:T(512)S(1)} %broadcast_multiply_fusion.1) | copy-start | bytes 6148
  15.2 73.5 %copy-start.31 = (f32[512]{0:T(512)}, f32[512]{0:T(512)S(1)}, u32[]{:S(2)}) copy-start(f32[512]{0:T(512)S(1)} %fusion.35) | copy-start | bytes 6148
  81.1 7.7 copy-start.27
  81.1 7.7 copy-start.46
  82.8 51.0 %copy-start.20 = (f32[512,10]{0,1:T(8,128)}, f32[512,10]{0,1:T(8,128)S(1)}, u32[]{:S(2)}) copy-start(f32[512,10]{0,1:T(8,128)S(1)} %get-tuple-element.286) | copy-start | bytes 61444
  82.8 51.0 %copy-start.22 = (f32[512,10]{0,1:T(8,128)}, f32[512,10]{0,1:T(8,128)S(1)}, u32[]{:S(2)}) copy-start(f32[512,10]{0,1:T(8,128)S(1)} %get-tuple-element.287) | copy-start | bytes 61444
  82.8 51.0 %copy-start.24 = (f32[512,10]{0,1:T(8,128)}, f32[512,10]{0,1:T(8,128)S(1)}, u32[]{:S(2)}) copy-start(f32[512,10]{0,1:T(8,128)S(1)} %get-tuple-element.288) | copy-start | bytes 61444
  92.6 34.2 %all-to-all-start.2 = ((bf16[512,2,512]{2,0,1:T(8,128)(2,1)}), bf16[512,2,512]{2,0,1:T(8,128)(2,1)S(1)}, u32[]{:S(2)}, u32[]{:S(2)}) async-start(bf16[512,2,512]{2,0,1:T(8,128)(2,1)} %bitcast.162), calls=%async_computation.2 | async-start | bytes 2097152 | tf_op jit(solution)/shard_map/all_to_all | solution.py:201
  126.8 30.2 %all-to-all-start.1 = ((bf16[512,2,512]{0,2,1:T(8,128)(2,1)}), bf16[512,2,512]{0,2,1:T(8,128)(2,1)}, u32[]{:S(2)}, u32[]{:S(2)}) async-start(bf16[512,2,512]{0,2,1:T(8,128)(2,1)} %bitcast.17), calls=%async_computation.1 | async-start | bytes 2097152 | tf_op jit(solution)/shard_map/all_to_all | solution.py:200
  156.9 14.3 %all-to-all-start = ((bf16[512,2,512]{0,2,1:T(8,128)(2,1)}), bf16[512,2,512]{0,2,1:T(8,128)(2,1)}, u32[]{:S(2)}, u32[]{:S(2)}) async-start(bf16[512,2,512]{0,2,1:T(8,128)(2,1)} %bitcast.14), calls=%async_computation | async-start | bytes 2097152 | tf_op jit(solution)/shard_map/all_to_all | solution.py:199
  171.2 32.1 %copy-start.64 = (bf16[256]{0:T(256)(128)(2,1)S(1)}, bf16[256]{0:T(256)(128)(2,1)}, u32[]{:S(2)}) copy-start(bf16[256]{0:T(256)(128)(2,1)} %param.30) | copy-start | bytes 1540
  171.2 32.1 %copy-start.55 = (bf16[1024]{0:T(1024)(128)(2,1)S(1)}, bf16[1024]{0:T(1024)(128)(2,1)}, u32[]{:S(2)}) copy-start(bf16[1024]{0:T(1024)(128)(2,1)} %get-tuple-element.208) | copy-start | bytes 6148
  171.2 32.2 %copy-start.54 = (bf16[1024]{0:T(1024)(128)(2,1)S(1)}, bf16[1024]{0:T(1024)(128)(2,1)}, u32[]{:S(2)}) copy-start(bf16[1024]{0:T(1024)(128)(2,1)} %get-tuple-element.207) | copy-start | bytes 6148
  171.2 32.2 %copy-start.53 = (bf16[1024]{0:T(1024)(128)(2,1)S(1)}, bf16[1024]{0:T(1024)(128)(2,1)}, u32[]{:S(2)}) copy-start(bf16[1024]{0:T(1024)(128)(2,1)} %get-tuple-element.206) | copy-start | bytes 6148
  171.2 51.0 %copy-start.3 = (bf16[1,512,1024]{2,1,0:T(8,128)(2,1)S(1)}, bf16[1,512,1024]{2,1,0:T(8,128)(2,1)}, u32[]{:S(2)}) copy-start(bf16[1,512,1024]{2,1,0:T(8,128)(2,1)} %param.19) | copy-start | bytes 3145732
  178.3 5.7 copy-start.18
  192.1 5.7 copy-start.18
  198.9 23.4 %all-to-all-start.3 = ((bf16[2,512,512]{1,2,0:T(8,128)(2,1)}), bf16[2,512,512]{1,2,0:T(8,128)(2,1)}, u32[]{:S(2)}, u32[]{:S(2)}) async-start(bf16[2,512,512]{1,2,0:T(8,128)(2,1)} %get-tuple-element.96), calls=%async_computation.3 | async-start | bytes 2097152 | tf_op jit(solution)/shard_map/all_to_all | solution.py:204
  203.4 87.2 %copy-start.41 = (f32[1024]{0:T(1024)}, f32[1024]{0:T(1024)S(1)}, u32[]{:S(2)}) copy-start(f32[1024]{0:T(1024)S(1)} %convert_element_type.175) | copy-start | bytes 12292
  203.4 25.7 %copy-start.48 = (f32[1024]{0:T(1024)}, f32[1024]{0:T(1024)S(1)}, u32[]{:S(2)}) copy-start(f32[1024]{0:T(1024)S(1)} %convert_element_type.176) | copy-start | bytes 12292
  226.8 63.7 %copy-start.37 = (f32[512]{0:T(512)}, f32[512]{0:T(512)S(1)}, u32[]{:S(2)}) copy-start(f32[512]{0:T(512)S(1)} %broadcast_multiply_fusion) | copy-start | bytes 6148
  229.0 61.5 %copy-start.43 = (f32[512]{0:T(512)}, f32[512]{0:T(512)S(1)}, u32[]{:S(2)}) copy-start(f32[512]{0:T(512)S(1)} %fusion.36) | copy-start | bytes 6148
  229.1 40.1 %copy-start.9 = (bf16[1,512,1024]{2,1,0:T(8,128)(2,1)S(1)}, bf16[1,512,1024]{2,1,0:T(8,128)(2,1)}, u32[]{:S(2)}) copy-start(bf16[1,512,1024]{2,1,0:T(8,128)(2,1)} %param.33) | copy-start | bytes 3145732
  269.2 12.6 %copy-start.56 = (bf16[1024,4096]{1,0:T(8,128)(2,1)S(1)}, bf16[1024,4096]{1,0:T(8,128)(2,1)}, u32[]{:S(2)}) copy-start(bf16[1024,4096]{1,0:T(8,128)(2,1)} %all-gather.10.cloned.1.call-done) | copy-start | bytes 25165828
  281.8 8.7 copy-start.65
  298.5 6.9 copy-start.14
  300.8 18.8 %all-to-all-start.4 = ((bf16[512,2,512]{0,2,1:T(8,128)(2,1)}), bf16[512,2,512]{0,2,1:T(8,128)(2,1)}, u32[]{:S(2)}, u32[]{:S(2)}) async-start(bf16[512,2,512]{0,2,1:T(8,128)(2,1)} %bitcast.25), calls=%async_computation.4 | async-start | bytes 2097152 | tf_op jit(solution)/shard_map/all_to_all | solution.py:252
  305.3 212.5 %reduce-scatter.7.cloned.1.call-start = ((), (), s32[]{:S(2)}) async-start(), calls=%async_computation.17 | async-start | bytes 4456448 | tf_op jit(solution)/shard_map/reduce_scatter | solution.py:284
  349.0 6.2 copy-start
  389.2 6.2 copy-start
  395.4 4.6 copy-start.16
  401.1 3.7 copy-start.1
  401.1 17.4 %all-to-all-start.5 = ((bf16[2,512,512]{1,2,0:T(8,128)(2,1)}), bf16[2,512,512]{1,2,0:T(8,128)(2,1)S(1)}, u32[]{:S(2)}, u32[]{:S(2)}) async-start(bf16[2,512,512]{1,2,0:T(8,128)(2,1)} %get-tuple-element.98), calls=%async_computation.5 | async-start | bytes 2097152 | tf_op jit(solution)/shard_map/all_to_all | solution.py:257
  405.9 16.2 %copy-start.26 = (f32[3,512,10]{1,2,0:T(8,128)S(1)}, f32[3,512,10]{1,2,0:T(8,128)}, u32[]{:S(2)}) copy-start(f32[3,512,10]{1,2,0:T(8,128)} %get-tuple-element.273) | copy-start | bytes 184324
  418.5 16.4 %all-to-all-start.6 = ((bf16[2,512,512]{1,2,0:T(8,128)(2,1)}), bf16[2,512,512]{1,2,0:T(8,128)(2,1)S(1)}, u32[]{:S(2)}, u32[]{:S(2)}) async-start(bf16[2,512,512]{1,2,0:T(8,128)(2,1)} %copy.62), calls=%async_computation.6 | async-start | bytes 2097152 | tf_op jit(solution)/shard_map/all_to_all | solution.py:258
  430.7 9.9 copy-start.21
  430.7 9.9 copy-start.23
  430.7 9.9 copy-start.25
  434.9 42.1 %all-to-all-start.7 = ((bf16[2,512,512]{1,2,0:T(8,128)(2,1)}), bf16[2,512,512]{1,2,0:T(8,128)(2,1)}, u32[]{:S(2)}, u32[]{:S(2)}) async-start(bf16[2,512,512]{1,2,0:T(8,128)(2,1)} %copy.63), calls=%async_computation.7 | async-start | bytes 2097152 | tf_op jit(solution)/shard_map/all_to_all | solution.py:259
  439.4 180.6 %reduce-scatter.5.cloned.1.call-start = ((), (), s32[]{:S(2)}) async-start(), calls=%async_computation.16 | async-start | bytes 13369344 | tf_op jit(solution)/shard_map/reduce_scatter | solution.py:282
  462.2 14.8 %copy-start.4 = (bf16[1,512,1024]{2,1,0:T(8,128)(2,1)S(1)}, bf16[1,512,1024]{2,1,0:T(8,128)(2,1)}, u32[]{:S(2)}) copy-start(bf16[1,512,1024]{2,1,0:T(8,128)(2,1)} %param.19) | copy-start | bytes 3145732
  462.2 14.8 %copy-start.28 = (f32[1024]{0:T(1024)S(1)}, f32[1024]{0:T(1024)}, u32[]{:S(2)}) copy-start(f32[1024]{0:T(1024)} %copy-done.27) | copy-start | bytes 12292
  462.2 14.9 %copy-start.30 = (f32[512]{0:T(512)S(1)}, f32[512]{0:T(512)}, u32[]{:S(2)}) copy-start(f32[512]{0:T(512)} %copy-done.29) | copy-start | bytes 6148
  462.2 14.9 %copy-start.32 = (f32[512]{0:T(512)S(1)}, f32[512]{0:T(512)}, u32[]{:S(2)}) copy-start(f32[512]{0:T(512)} %copy-done.31) | copy-start | bytes 6148
  462.2 14.9 %copy-start.47 = (f32[1024]{0:T(1024)S(1)}, f32[1024]{0:T(1024)}, u32[]{:S(2)}) copy-start(f32[1024]{0:T(1024)} %copy-done.46) | copy-start | bytes 12292
  486.9 315.4 %reduce-scatter.9.cloned.1.call-start = ((), (), s32[]{:S(2)}) async-start(), calls=%async_computation.18 | async-start | bytes 17825792 | tf_op jit(solution)/shard_map/reduce_scatter | solution.py:288
  503.4 481.2 %reduce-scatter.11.cloned.1.call-start = ((), (), s32[]{:S(2)}) async-start(), calls=%async_computation.19 | async-start | bytes 17825792 | tf_op jit(solution)/shard_map/reduce_scatter | solution.py:290
  515.7 557.8 %all-reduce.21.cloned.1.call-start = ((), (), s32[]{:S(2)}) async-start(), calls=%async_computation.20 | async-start | bytes 6291456 | tf_op jit(solution)/shard_map/psum | solution.py:294
  984.6 10.7 copy-start.11
  995.3 7.0 copy-start.36
  1073.5 6.1 copy-start.15
  (24 other events, 40.9 us)
Sparse Core Ops, SparseCore 0:
  10.4 65.2 all-gather.5
  77.8 40.0 all-gather.7
  120.1 73.6 all-gather.9
  195.8 73.3 all-gather.11
  310.0 71.0 reduce-scatter.6
  487.1 132.8 reduce-scatter.4
  624.6 177.6 reduce-scatter.8
  807.0 177.5 reduce-scatter.10
  987.2 85.3 all-reduce.20
where the time goes:
time: 1100 us; the launch traced here: 1090 us
  waiting for transfers between devices  526 us (48%)
  matrix products  173 us (16%)
  blocking collectives  148 us (13%)
  local copies, waits for them, and re-layouts  130 us (12%)
  other arithmetic  56.9 us (5%)
  starting transfers between devices  34.1 us (3%)
  between operations  18.4 us (2%)
    reduce_scatter x1, waiting for transfers between devices, on_device(): lax.psum_scatter(up_grad, 'fsdp', scatter_dimension=0, tiled=True)  182 us
    reduce_scatter x1, waiting for transfers between devices, on_device(): lax.psum_scatter(down_grad, 'fsdp', scatter_dimension=0, tiled=True)  182 us
    unnamed x2, blocking collectives  124 us
    reduce_scatter x1, waiting for transfers between devices, on_device(): lax.psum_scatter(qkv_w_grad, 'fsdp', scatter_dimension=0, tiled=True)  102 us
    concatenate x4, local copies, waits for them, and re-layouts, rotate(): return jnp.concatenate(pieces, axis=-1)  72.6 us
    all_gather x1, waiting for transfers between devices, on_device(): lax.all_gather(fc2_weight, 'fsdp', axis=0, tiled=True)  28.7 us
  transfers between devices with their start and end apart: 17, of which 8 were waited for; matrix products, arithmetic and copies ran while one was open for 29% of the time, Pallas kernels for 0%

commit v1 on v0

v1 whole, which is shorter than its diff:
```python
import functools

import jax
import jax.numpy as jnp
import numpy as np
from jax import lax
from jax.experimental import pallas as pl
from jax.experimental.pallas import tpu as pltpu
from jax.sharding import PartitionSpec as P

HD = 64
EPS = 1e-06
THETA = 10000.0
LOG2E = 1.4426950408889634
SCALE = HD**-0.5
BF = jnp.bfloat16
F32 = jnp.float32
NT = (((1,), (1,)), ((), ()))
TN = (((0,), (0,)), ((), ()))
NN = (((1,), (0,)), ((), ()))
SMALL = 128
VMEM_BYTES = 56 << 20
SHARD = "fsdp"
SEQ = "seq"


def mm(a, b, dims=NN):
    return lax.dot_general(a, b, dims, preferred_element_type=F32)


def shifted(size, by):
    return [(i, (i + by) % size) for i in range(size)]


def take(values, index, axis):
    return lax.dynamic_index_in_dim(values, index, axis, keepdims=False)


def shape(dims, dtype):
    return jax.ShapeDtypeStruct(dims, dtype)


def fixed(*dims):
    return pl.BlockSpec(dims, lambda *_: (0,) * len(dims))


def call(kernel, grid, in_specs, out_specs, out_shape, flops, moved, exps=0, scratch=()):
    return pl.pallas_call(
        kernel,
        grid=grid,
        in_specs=in_specs,
        out_specs=out_specs,
        out_shape=out_shape,
        scratch_shapes=list(scratch),
        compiler_params=pltpu.CompilerParams(vmem_limit_bytes=VMEM_BYTES),
        cost_estimate=pl.CostEstimate(flops=flops, bytes_accessed=moved, transcendentals=exps),
    )


def rotated(values, cos, low, high):
    half = 2 * (HD // 3 // 2) // 2
    return values * cos + pltpu.roll(values, values.shape[1] - half, 1) * low + pltpu.roll(values, half, 1) * high


def project_kernel(x_ref, w_ref, b_ref, cos_ref, low_ref, high_ref, out_ref):
    values = mm(x_ref[...], w_ref[...]) + b_ref[...]
    width = values.shape[1]

    @pl.when(pl.program_id(0) < 2)
    def _():
        cos, low, high = cos_ref[...], low_ref[...], high_ref[...]
        for j in range(0, width, 128):
            out_ref[:, j : j + 128] = rotated(values[:, j : j + 128], cos, low, high).astype(BF)

    @pl.when(pl.program_id(0) >= 2)
    def _():
        out_ref[...] = values.astype(BF)


def project(x, weight, bias, tables, width):
    rows, depth = x.shape
    start = depth // width
    return call(
        project_kernel,
        (3,),
        [
            fixed(rows, depth),
            pl.BlockSpec((depth, width), lambda i: (0, start + i)),
            pl.BlockSpec((1, width), lambda i: (0, i)),
        ]
        + [fixed(rows, 128)] * 3,
        pl.BlockSpec((rows, width), lambda i: (0, i)),
        shape((rows, 3 * width), BF),
        6 * rows * depth * width,
        6 * depth * width + 2 * rows * (depth + 3 * width),
    )(x, weight, bias, *tables)


def rotary_tables(positions):
    width = 2 * (HD // 3 // 2)
    half = width // 2
    freqs = np.power(np.float32(THETA), -(np.arange(half, dtype=np.float32) * np.float32(2.0 / width)))
    column = np.arange(2 * HD) % HD
    turns = column < 3 * width
    axis = np.minimum(column // width, 2)
    freq = np.where(turns, freqs[column % half], 0.0).astype(np.float32)
    leading = turns & (column % width < half)
    trailing = turns & (column % width >= half)
    place = jnp.where(axis == 0, positions[0][:, None], jnp.where(axis == 1, positions[1][:, None], positions[2][:, None]))
    angle = place * freq
    sine = jnp.sin(angle)
    return jnp.cos(angle), jnp.where(leading, -sine, 0.0), jnp.where(trailing, sine, 0.0)


def over_blocks(rows, block, step):
    if rows // block <= 4:
        for i in range(rows // block):
            step(pl.ds(i * block, block))
    else:

        def body(i, carry):
            step(pl.ds(pl.multiple_of(i * block, block), block))
            return carry

        lax.fori_loop(0, rows // block, body, 0)


def attend_kernel(block, q_ref, k_ref, v_ref, o_ref, lse_ref):
    rows = q_ref.shape[0]
    first = lax.broadcasted_iota(jnp.int32, (1, 128), 1) < HD
    factor = jnp.float32(SCALE * LOG2E)
    zero = jnp.zeros((), BF)

    def step(rs):
        q = q_ref[rs, :]
        outs, lses = [], []
        for h in range(2):
            mine = first if h == 0 else jnp.logical_not(first)
            scores = mm(jnp.where(mine, q, zero), k_ref[...], NT)
            peak = jnp.max(scores, axis=1, keepdims=True) * factor
            weights = jnp.exp2(scores * factor - peak)
            total = jnp.sum(weights, axis=1, keepdims=True)
            outs.append(mm(weights.astype(BF), v_ref[...]) * (1.0 / total))
            lses.append(peak + jnp.log2(total))
        o_ref[rs, :] = jnp.where(first, outs[0], outs[1]).astype(BF)
        lse_ref[rs, :] = jnp.where(first, lses[0], lses[1])

    over_blocks(rows, block, step)


def attend_back_kernel(
    block, q_ref, k_ref, v_ref, o_ref, lse_ref, do_ref, cos_ref, low_ref, high_ref, dq_ref, dk_ref, dv_ref, dk_sum, dv_sum
):
    rows = q_ref.shape[0]
    first = lax.broadcasted_iota(jnp.int32, (1, 128), 1) < HD
    factor = jnp.float32(SCALE * LOG2E)
    zero = jnp.zeros((), BF)
    dk_sum[...] = jnp.zeros_like(dk_sum)
    dv_sum[...] = jnp.zeros_like(dv_sum)

    def step(rs):
        q, do = q_ref[rs, :], do_ref[rs, :]
        od = o_ref[rs, :].astype(F32) * do.astype(F32)
        lse = lse_ref[rs, :]
        dq = None
        for h in range(2):
            mine = first if h == 0 else jnp.logical_not(first)
            qh, doh = jnp.where(mine, q, zero), jnp.where(mine, do, zero)
            delta = jnp.sum(jnp.where(mine, od, 0.0), axis=1, keepdims=True)
            k = k_ref[...]
            p = jnp.exp2(mm(qh, k, NT) * factor - lse[:, h * HD : h * HD + 1])
            ds = (p * (mm(doh, v_ref[...], NT) - delta)).astype(BF)
            dv_sum[...] += mm(p.astype(BF), doh, TN)
            dk_sum[...] += mm(ds, qh, TN)
            part = mm(ds, jnp.where(mine, k, zero))
            dq = part if dq is None else dq + part
        dq = (dq * SCALE).astype(BF).astype(F32)
        dq_ref[rs, :] = rotated(dq, cos_ref[rs, :], -low_ref[rs, :], -high_ref[rs, :]).astype(BF)

    over_blocks(rows, block, step)
    dk = (dk_sum[...] * SCALE).astype(BF).astype(F32)
    dk_ref[...] = rotated(dk, cos_ref[...], -low_ref[...], -high_ref[...]).astype(BF)
    dv_ref[...] = dv_sum[...].astype(BF)


def pair_spec(rows, first=0):
    return pl.BlockSpec((rows, 128), lambda i: (0, first + i))


def attend(qkv, block=512):
    rows, columns = qkv.shape[0], qkv.shape[1] // 3
    pairs = columns // 128
    return call(
        functools.partial(attend_kernel, min(block, (1 << 19) // rows)),
        (pairs,),
        [pair_spec(rows, k * pairs) for k in range(3)],
        [pair_spec(rows)] * 2,
        [shape((rows, columns), BF), shape((rows, columns), F32)],
        16 * rows * rows * columns,
        rows * columns * 12,
        rows * rows * columns // HD,
    )(qkv, qkv, qkv)


def attend_back(qkv, o, lse, do, tables, block=512):
    rows, columns = o.shape
    pairs = columns // 128
    return call(
        functools.partial(attend_back_kernel, min(block, (1 << 19) // rows)),
        (pairs,),
        [pair_spec(rows, k * pairs) for k in range(3)] + [pair_spec(rows)] * 3 + [fixed(rows, 128)] * 3,
        [pair_spec(rows)] * 3,
        [shape((rows, columns), BF)] * 3,
        40 * rows * rows * columns,
        rows * columns * 20,
        rows * rows * columns // HD,
        [pltpu.VMEM((rows, 128), F32)] * 2,
    )(qkv, qkv, qkv, o, lse, do, *tables)


def normalise(values):
    center = values - jnp.mean(values, axis=-1, keepdims=True)
    factor = lax.rsqrt(jnp.mean(center * center, axis=-1, keepdims=True) + EPS)
    return center * factor, factor


def normalise_back(grads, gain, normal, factor):
    e = grads * gain
    inner = e - jnp.mean(e, axis=-1, keepdims=True) - normal * jnp.mean(e * normal, axis=-1, keepdims=True)
    return factor * inner


def column_sums(out_ref, *parts):
    sums = [jnp.sum(p, axis=0, keepdims=True) for p in parts]
    sums.append(jnp.zeros((8 - len(sums), sums[0].shape[1]), F32))
    block = jnp.concatenate(sums, axis=0)

    @pl.when(pl.program_id(0) == 0)
    def _():
        out_ref[...] = block

    @pl.when(pl.program_id(0) > 0)
    def _():
        out_ref[...] += block


def out_kernel(att_ref, w_ref, tokens_ref, b_ref, gain_ref, bias_ref, hidden_ref, normed_ref):
    hidden = tokens_ref[...].astype(F32) + mm(att_ref[...], w_ref[...]) + b_ref[...]
    hidden_ref[...] = hidden
    normed_ref[...] = (normalise(hidden)[0] * gain_ref[...] + bias_ref[...]).astype(BF)


def project_out(att, weight, tokens, b, gain, bias, block=256):
    rows, width = tokens.shape
    row = pl.BlockSpec((block, width), lambda i: (i, 0))
    return call(
        out_kernel,
        (rows // block,),
        [row, fixed(width, width), row] + [fixed(1, width)] * 3,
        [row, row],
        [shape((rows, width), F32), shape((rows, width), BF)],
        2 * rows * width * width,
        2 * width * width + 10 * rows * width,
    )(att, weight, tokens, b, gain, bias)


def hidden_back_kernel(extra, *refs):
    dn_ref, far_refs, (hidden_ref, og_ref, gain_ref, w_ref, grad_ref, branch_ref, att_ref, sums_ref) = (
        refs[0],
        refs[1 : 1 + extra],
        refs[1 + extra :],
    )
    dn = dn_ref[...]
    for far in far_refs:
        dn = dn + far[...].astype(F32)
    normal, factor = normalise(hidden_ref[...])
    og = og_ref[...].astype(F32)
    grad = og + normalise_back(dn, gain_ref[...], normal, factor)
    grad_ref[...] = grad
    branch = grad.astype(BF)
    branch_ref[...] = branch
    att_ref[...] = mm(branch, w_ref[...], NT).astype(BF)
    column_sums(sums_ref, dn * normal, dn, branch.astype(F32), og)


def hidden_back(dn, dn_far, hidden, og, gain, weight, block=256):
    rows, width = hidden.shape
    row = pl.BlockSpec((block, width), lambda i: (i, 0))
    return call(
        functools.partial(hidden_back_kernel, len(dn_far)),
        (rows // block,),
        [row] * (1 + len(dn_far)) + [row, row, fixed(1, width), fixed(width, width)],
        [row, row, row, fixed(8, width)],
        [shape((rows, width), F32), shape((rows, width), BF), shape((rows, width), BF), shape((8, width), F32)],
        2 * rows * width * width,
        2 * width * width + 18 * rows * width,
    )(dn, *dn_far, hidden, og, gain, weight)


def tokens_back_kernel(extra, *refs):
    dn_ref, far_refs, (tokens_ref, grad_ref, gain_ref, out_ref) = refs[0], refs[1 : 1 + extra], refs[1 + extra :]
    dn = dn_ref[...]
    for far in far_refs:
        dn = dn + far[...].astype(F32)
    normal, factor = normalise(tokens_ref[...].astype(F32))
    out_ref[...] = grad_ref[...] + normalise_back(dn, gain_ref[...], normal, factor)


def tokens_back(dn, dn_far, tokens, grad, gain, block=256):
    rows, width = tokens.shape
    row = pl.BlockSpec((block, width), lambda i: (i, 0))
    return call(
        functools.partial(tokens_back_kernel, len(dn_far)),
        (rows // block,),
        [row] * (3 + len(dn_far)) + [fixed(1, width)],
        row,
        shape((rows, width), F32),
        20 * rows * width,
        14 * rows * width,
    )(dn, *dn_far, tokens, grad, gain)


def project_back_kernel(dq_ref, dk_ref, dv_ref, wq_ref, wk_ref, wv_ref, tokens_ref, out_ref, sums_ref):
    total = mm(dq_ref[...], wq_ref[...], NT) + mm(dk_ref[...], wk_ref[...], NT) + mm(dv_ref[...], wv_ref[...], NT)
    out_ref[...] = total.astype(out_ref.dtype)
    normal, _ = normalise(tokens_ref[...].astype(F32))
    column_sums(sums_ref, total * normal, total)


def project_back(grads, weight, tokens, piece, dtype):
    rows = tokens.shape[0]
    width = grads[0].shape[1]
    depth = weight.shape[0]
    start = depth // width
    block = rows // 2
    part = pl.BlockSpec((block, width), lambda i: (2 * piece + i, 0))
    row = pl.BlockSpec((block, depth), lambda i: (i, 0))
    return call(
        project_back_kernel,
        (2,),
        [part] * 3 + [pl.BlockSpec((depth, width), lambda i, k=k: (0, start + k)) for k in range(3)] + [row],
        [row, fixed(8, depth)],
        [shape((rows, depth), dtype), shape((8, depth), F32)],
        6 * rows * width * depth,
        6 * depth * width + 6 * rows * width + 6 * rows * depth,
    )(*grads, weight, weight, weight, tokens)


def unpack_down(block, rows, width):
    parts = block.shape[1] // width
    if parts == 1:
        return block
    owners = block.shape[0] // rows
    return jnp.concatenate(
        [block[f * rows : (f + 1) * rows, j * width : (j + 1) * width] for f in range(owners) for j in range(parts)], axis=0
    )


def feed_kernel(owned, x_ref, og_ref, up_ref, down_ref, b_ref, act_ref, pre_ref, dn_ref, out_ref, sums_ref, dn_sum, out_sum):
    step, last = pl.program_id(0), pl.num_programs(0) - 1
    width = x_ref.shape[1]
    up = up_ref[...]
    down = unpack_down(down_ref[...], owned, width)
    u = mm(x_ref[...], up) + b_ref[...]
    phi = 0.5 * (1.0 + lax.erf(u * 0.7071067811865476))
    slope = phi + u * jnp.exp(-0.5 * u * u) * 0.3989422804014327
    act = (u * phi).astype(BF)
    act_ref[...] = act
    pre = (mm(og_ref[...], down, NT) * slope).astype(BF)
    pre_ref[...] = pre
    sums_ref[...] = jnp.sum(pre.astype(F32), axis=0, keepdims=True)
    dn = mm(pre, up, NT)
    out = mm(act, down)

    @pl.when(step == 0)
    def _():
        dn_sum[...] = dn
        out_sum[...] = out

    @pl.when(step > 0)
    def _():
        dn_sum[...] += dn
        out_sum[...] += out

    @pl.when(step == last)
    def _():
        dn_ref[...] = dn_sum[...].astype(dn_ref.dtype)
        out_ref[...] = out_sum[...].astype(out_ref.dtype)


def feed(x, og, up, down, bias, owned, dtype, block=512):
    rows, width = x.shape
    hidden = bias.shape[1]
    block = min(block, hidden)
    steps = hidden // block
    down_rows = down.shape[0] // steps
    down_columns = hidden if down.shape[1] > width else width
    columns = pl.BlockSpec((rows, block), lambda i: (0, i))
    vector = pl.BlockSpec((1, block), lambda i: (0, i))
    return call(
        functools.partial(feed_kernel, owned),
        (steps,),
        [
            fixed(rows, width),
            fixed(rows, width),
            pl.BlockSpec((width, block), lambda i: (0, i)),
            pl.BlockSpec((down_rows, down_columns), lambda i: (i, down.shape[1] // down_columns - 1)),
            vector,
        ],
        [columns, columns, fixed(rows, width), fixed(rows, width), vector],
        [
            shape((rows, hidden), BF),
            shape((rows, hidden), BF),
            shape((rows, width), dtype),
            shape((rows, width), dtype),
            shape((1, hidden), F32),
        ],
        8 * rows * width * hidden,
        4 * width * hidden + rows * (4 * hidden + 8 * width),
        2 * rows * hidden,
        [pltpu.VMEM((rows, width), F32)] * 2,
    )(x, og, up, down, bias)


def feed_grad_kernel(owned, count, *refs):
    xs, pres, acts, ogs = (refs[k * count : (k + 1) * count] for k in range(4))
    out_ref = refs[4 * count]
    ups = pl.num_programs(0) // 2
    step = pl.program_id(0)

    @pl.when(step < ups)
    def _():
        out_ref[...] = functools.reduce(jnp.add, [mm(x[...], p[...], TN) for x, p in zip(xs, pres)]).astype(BF)

    @pl.when(step >= ups)
    def _():
        grad = functools.reduce(jnp.add, [mm(a[...], g[...], TN) for a, g in zip(acts, ogs)]).astype(BF)
        width = grad.shape[1]
        parts = out_ref.shape[1] // width
        for f in range(out_ref.shape[0] // owned):
            for j in range(parts):
                start = (f * parts + j) * owned
                out_ref[f * owned : (f + 1) * owned, j * width : (j + 1) * width] = grad[start : start + owned, :]


def feed_grad(xs, pres, acts, ogs, owned, block=256):
    rows, width = xs[0].shape
    hidden = pres[0].shape[1]
    ups = width // block
    tall = block * hidden // width
    first = lambda i: (0, jnp.minimum(i, ups - 1))
    second = lambda i: (0, jnp.maximum(i - ups, 0))
    count = len(xs)
    return call(
        functools.partial(feed_grad_kernel, owned, count),
        (2 * ups,),
        [pl.BlockSpec((rows, block), first)] * count
        + [fixed(rows, hidden)] * count
        + [pl.BlockSpec((rows, tall), second)] * count
        + [fixed(rows, width)] * count,
        pl.BlockSpec((block, hidden), lambda i: (lax.rem(i, ups), lax.div(i, ups))),
        shape((width, 2 * hidden), BF),
        4 * count * rows * width * hidden,
        count * rows * (4 * width + 4 * hidden) + 4 * width * hidden,
    )(*xs, *pres, *acts, *ogs)


def attention_grad_kernel(att_ref, branch_ref, x_ref, dq_ref, dk_ref, dv_ref, small_ref, out_ref):
    width, n = branch_ref.shape[1], dq_ref.shape[1]
    out_ref[:, :width] = mm(att_ref[...], branch_ref[...], TN).astype(BF)
    x = x_ref[...]
    for k, ref in enumerate((dq_ref, dk_ref, dv_ref)):
        out_ref[:, width + k * n : width + (k + 1) * n] = mm(x, ref[...], TN).astype(BF)
    out_ref[:, width + 3 * n :] = small_ref[...].T.astype(BF)


def attention_grad(att, branch, x, grads, small, block=256):
    rows, depth = x.shape
    own = att.shape[0]
    width = grads[0].shape[1]
    columns = depth + 3 * width + SMALL
    return call(
        attention_grad_kernel,
        (depth // block,),
        [pl.BlockSpec((own, block), lambda i: (0, i)), fixed(own, depth), pl.BlockSpec((rows, block), lambda i: (0, i))]
        + [fixed(rows, width)] * 3
        + [pl.BlockSpec((SMALL, block), lambda i: (0, i))],
        pl.BlockSpec((block, columns), lambda i: (i, 0)),
        shape((depth, columns), BF),
        6 * rows * depth * width + 2 * own * depth * depth,
        2 * rows * (depth + 3 * width) + 2 * depth * columns,
    )(att, branch, x, *grads, small)


def after(values, *earlier):
    return lax.optimization_barrier((values, earlier))[0]


def on_device(
    tokens, positions, ln1_gain, ln1_bias, qkv_weight, qkv_bias, out_weight, out_bias,
    ln2_gain, ln2_bias, fc1_weight, fc1_bias, fc2_weight, fc2_bias, out_grad,
):
    rows, width = tokens.shape[1], tokens.shape[2]
    depth = qkv_weight.shape[0]
    owners, group = width // depth, lax.axis_size(SEQ)
    me, side = lax.axis_index(SHARD), lax.axis_index(SEQ)
    others = range(1, group)
    heads = width // group
    hidden_owned = fc2_weight.shape[0] // group
    packs = hidden_owned % depth == 0

    def gather(values):
        return lax.all_gather(values, SHARD, axis=0, tiled=True)

    def scatter(values):
        return lax.psum_scatter(values, SHARD, scatter_dimension=0, tiled=True)

    def spread(values):
        return [values] + [lax.ppermute(values, SEQ, shifted(group, d)) for d in others]

    def in_order(parts):
        stacked = jnp.stack(parts)
        return [take(stacked, (k - side) % group, 0) for k in range(group)]

    own_qkv = take(qkv_weight.reshape(depth, 3, group, heads), side, 2).reshape(depth, 3 * heads)
    names = (ln1_gain, ln1_bias, out_bias, ln2_gain, ln2_bias, fc2_bias, qkv_bias, fc1_bias)
    columns = [p.reshape(-1, depth).T for p in names]
    counts = [c.shape[1] for c in columns]
    extra = jnp.pad(jnp.concatenate(columns, axis=1), ((0, 0), (0, SMALL - sum(counts))))
    w_att = gather(jnp.concatenate([out_weight, own_qkv, extra], axis=1))
    own_up = take(fc1_weight.reshape(depth, owners, group, hidden_owned), side, 2).reshape(depth, -1)
    own_down = take(fc2_weight.reshape(group, hidden_owned, width), side, 0)
    if packs:
        own_down = own_down.reshape(-1, depth, width).transpose(1, 0, 2).reshape(depth, -1)
        w_up = w_down = gather(jnp.concatenate([own_up, own_down], axis=1))
    else:
        w_up, w_down = gather(own_up), gather(own_down)

    clip = spread(tokens[0])
    places = jnp.concatenate(spread(positions[:, 0, :].astype(F32)), axis=1)
    grads = spread(out_grad[0])

    tables = rotary_tables(places)
    normal_one, _ = normalise(jnp.concatenate(clip, axis=0).astype(F32))

    start = width + 3 * heads
    lines = w_att[:, start : start + SMALL].astype(F32).T[: sum(counts)]
    vectors, at = [], 0
    for n in counts:
        vectors.append(lines[at : at + n].reshape(n, owners, depth).transpose(1, 0, 2).reshape(1, -1))
        at += n
    gain_one, bias_one, b_out, gain_two, bias_two, b_down, b_qkv, b_up = vectors
    b_qkv = take(b_qkv.reshape(3, group, heads), side, 1).reshape(1, -1)
    b_up = take(b_up.reshape(owners, group, hidden_owned), side, 1).reshape(1, -1)

    normed_one = after((normal_one * gain_one + bias_one).astype(BF), grads)
    qkv = project(normed_one, w_att, b_qkv, tables, heads)
    att, lse = attend(qkv)

    mine = [att[:rows]] + [lax.ppermute(att[d * rows : (d + 1) * rows], SEQ, shifted(group, -d)) for d in others]
    att_rows = jnp.concatenate(in_order(mine), axis=1)
    hidden, normed_two = project_out(att_rows, w_att, tokens[0], b_out, gain_two, bias_two)
    normed = spread(normed_two)

    fed = [feed(x, g, w_up, w_down, b_up, depth, F32 if d == 0 else BF) for d, (x, g) in enumerate(zip(normed, grads))]
    acts, pres, dns, outs, sums = zip(*fed)
    dn_far = [lax.ppermute(dns[d], SEQ, shifted(group, -d)) for d in others]
    out_far = [lax.ppermute(outs[d], SEQ, shifted(group, -d)) for d in others]

    if packs:
        fed_grads = feed_grad(normed, pres, acts, grads, depth)
        fed_sum = scatter(fed_grads)
        dns = (after(dns[0], fed_grads),) + dns[1:]
    hidden_grad, branch, att_grad, sums_two = hidden_back(dns[0], dn_far, hidden, out_grad[0], gain_two, w_att)
    shares = att_grad.reshape(rows, group, heads)
    att_grads = [take(shares, side, 1)]
    att_grads += [lax.ppermute(take(shares, (side + d) % group, 1), SEQ, shifted(group, d)) for d in others]

    qkv_grads = attend_back(qkv, att, lse, jnp.concatenate(att_grads, axis=0), tables)
    parts_one = [project_back(qkv_grads, w_att, clip[d], d, F32 if d == 0 else BF) for d in range(group)]
    dn_one, sums_one = zip(*parts_one)
    dn_one_far = [lax.ppermute(dn_one[d], SEQ, shifted(group, -d)) for d in others]

    here = (jnp.arange(group) == side).astype(F32)
    qkv_b = jnp.stack([jnp.sum(g.astype(F32), axis=0) for g in qkv_grads])[:, None, :] * here[None, :, None]
    up_b = functools.reduce(jnp.add, sums).reshape(owners, 1, hidden_owned) * here[None, :, None]
    sums_one = functools.reduce(jnp.add, sums_one)
    vectors = (sums_one[0], sums_one[1], sums_two[2], sums_two[0], sums_two[1], sums_two[3], qkv_b, up_b)
    lines = [v.reshape(owners, n, depth).transpose(1, 0, 2).reshape(n, width) for v, n in zip(vectors, counts)]
    lines = jnp.pad(jnp.concatenate(lines, axis=0), ((0, SMALL - sum(counts)), (0, 0)))
    att_grads = attention_grad(att_rows, branch, normed_one, qkv_grads, lines)
    att_sum = scatter(after(att_grads, fed_sum) if packs else att_grads)
    tokens_grad = tokens_back(dn_one[0], dn_one_far, tokens[0], hidden_grad, gain_one)

    block_out = hidden + outs[0] + b_down
    for far in out_far:
        block_out = block_out + far.astype(F32)

    if packs:
        up_sum, down_sum = fed_sum[:, : own_up.shape[1]], fed_sum[:, own_up.shape[1] :]
        down_sum = down_sum.reshape(depth, -1, width).transpose(1, 0, 2).reshape(-1, width)
    else:
        up_sum = scatter(functools.reduce(jnp.add, [mm(x, p, TN) for x, p in zip(normed, pres)]).astype(BF))
        down_sum = scatter(functools.reduce(jnp.add, [mm(a, g, TN) for a, g in zip(acts, grads)]).astype(BF))

    def joined(values):
        return in_order([values] + [lax.ppermute(values, SEQ, shifted(group, -d)) for d in others])

    att_all = joined(att_sum)
    once = functools.reduce(jnp.add, [v.astype(F32) for v in att_all])
    out_total, columns = once[:, :width], once[:, width + 3 * heads :]
    qkv_total = jnp.stack([v[:, width : width + 3 * heads].reshape(depth, 3, heads) for v in att_all], axis=2)
    qkv_total = qkv_total.reshape(depth, -1).astype(F32)
    up_total = jnp.stack([v.reshape(depth, owners, hidden_owned) for v in joined(up_sum)], axis=2).reshape(depth, -1).astype(F32)
    down_total = jnp.concatenate(joined(down_sum), axis=0).astype(F32)

    lines, ends = columns.T, np.cumsum(counts)
    g1, b1, bo, g2, b2, bd, bq, bu = [lines[e - n : e].reshape(-1) for e, n in zip(ends, counts)]
    return (
        block_out.astype(BF)[None], tokens_grad[None], g1, b1, qkv_total, bq, out_total, bo, g2, b2, up_total, bu,
        down_total, bd,
    )


def solution(mesh):
    vector, matrix, tokens = P(SHARD), P(SHARD, None), P(SHARD, SEQ, None)
    return jax.shard_map(
        on_device,
        mesh=mesh,
        in_specs=(
            tokens, P(None, SHARD, SEQ), vector, vector, matrix, vector, matrix, vector, vector, vector, matrix, vector,
            matrix, vector, tokens,
        ),
        out_specs=(
            tokens, tokens, vector, vector, matrix, vector, matrix, vector, vector, vector, matrix, vector, matrix, vector
        ),
        check_vma=False,
    )
```

time: 1100 us -> 415 us (0.38)
  waiting for transfers between devices: 526 us -> 183 us
  matrix products: 173 us -> 0 us
  blocking collectives: 148 us -> 0 us
  Pallas kernels: 0 us -> 143 us
  local copies, waits for them, and re-layouts: 130 us -> 30.2 us
  other arithmetic: 56.9 us -> 21.7 us
  starting transfers between devices: 34.1 us -> 17.7 us
    reduce_scatter x4 -> x2, waiting for transfers between devices: 467 us -> 22.5 us  [scatter(): return lax.psum_scatter(values, SHARD, scatter_dimension=0, tiled=True)]
    dot_general x26 -> x0, matrix products: 173 us -> none  [the longest x2 19.5 us: one_block(): jnp.einsum('qhd,khd->hqk', grad_block, values_all, preferred_element_type...]
    pallas_call x0 -> x12, Pallas kernels: none -> 143 us  [the longest x2 33 us: feed(): call(functools.partial(feed_kernel, owned), (steps,), [fixed(rows, width)...]
    unnamed x2 -> x0, blocking collectives: 124 us -> none
    ppermute x0 -> x12, waiting for transfers between devices: none -> 115 us  [the longest x1 23.9 us: on_device(): dn_far = [lax.ppermute(dns[d], SEQ, shifted(group, -d)) for d in others]]
    concatenate x4 -> x3, local copies, waits for them, and re-layouts: 72.6 us -> 1.15 us  [the longest x2 0.98 us: on_device(): jnp.concatenate(columns, axis=1)]
    all_to_all x8 -> x0, starting transfers between devices: 33.3 us -> none  [the longest x1 4.65 us: on_device(): lax.all_to_all(queries, 'seq', split_axis=1, concat_axis=0, tiled=True)]
    all_to_all x8 -> x0, waiting for transfers between devices: 27.6 us -> none  [the longest x1 9.8 us: on_device(): lax.all_to_all(attended_grad, 'seq', split_axis=1, concat_axis=0, tiled=T...]
  transfers between devices with their start and end apart: 17 -> 16, of which waited for: 8 -> 10; matrix products, arithmetic and copies ran while one was open for 29% -> 9% of each run, Pallas kernels for 0% -> 27%
where the time goes in v1:
time: 415 us; the launch traced here: 411 us
  waiting for transfers between devices  183 us (44%)
  Pallas kernels  143 us (34%)
  local copies, waits for them, and re-layouts  30.2 us (7%)
  other arithmetic  21.7 us (5%)
  starting transfers between devices  17.7 us (4%)
  between operations  14.5 us (3%)
    all_gather x2, waiting for transfers between devices, gather(): return lax.all_gather(values, SHARD, axis=0, tiled=True)  45.7 us
    pallas_call x2, Pallas kernels, feed(): call(functools.partial(feed_kernel, owned), (steps,), [fixed(rows, width)...  33 us
    pallas_call x1, Pallas kernels, attend_back(): call(functools.partial(attend_back_kernel, min(block, (1 << 19) // rows))...  30.5 us
    ppermute x1, waiting for transfers between devices, on_device(): dn_far = [lax.ppermute(dns[d], SEQ, shifted(group, -d)) for d in others]  23.9 us
    ppermute x1, waiting for transfers between devices, on_device(): out_far = [lax.ppermute(outs[d], SEQ, shifted(group, -d)) for d in others]  22.7 us
    reduce_scatter x2, waiting for transfers between devices, scatter(): return lax.psum_scatter(values, SHARD, scatter_dimension=0, tiled=True)  22.5 us
    ppermute x4, waiting for transfers between devices, spread(): lax.ppermute(values, SEQ, shifted(group, d))  22.1 us
    ppermute x1, waiting for transfers between devices, on_device(): lax.ppermute(dn_one[d], SEQ, shifted(group, -d))  19.3 us
  transfers between devices with their start and end apart: 16, of which 10 were waited for; matrix products, arithmetic and copies ran while one was open for 9% of the time, Pallas kernels for 27%

profile of v1, /device:TPU:0, one launch (start us, length us, event | category | flops | bytes accessed | tf_op | source)
XLA Modules:
  0.0 410.5 jit_solution(423617741480699789)
XLA Ops:
  7.3 0.8 reshape.153
  8.1 0.7 reshape.154
  8.8 0.9 concatenate.29
  9.8 1.3 reshape.151
  11.1 1.3 dynamic-slice_reduce_fusion.1
  12.4 1.7 fusion.15
  14.7 1.5 dynamic-slice_reduce_fusion
  16.3 0.8 pad_maximum_fusion.3
  17.4 3.0 collective-permute-start
  20.6 2.0 collective-permute-start.1
  22.6 22.0 %collective-permute-done.2 = f32[3,512]{1,0:T(4,128)S(1)} collective-permute-done((f32[3,512]{1,0:T(4,128)S(1)}, f32[3,512]{1,0:T(4,128)S(1)}, u32[]{:S(2)}, u32[]{:S(2)}) %collective-permute-start.2) | collective-permute-done | bytes 6176 | tf_op jit(solution)/shard_map/ppermute | solution.py:519
  44.7 3.6 fusion.14
  48.6 0.7 fusion.2
  49.3 25.1 %all-gather.3.cloned.1.call-done.w_ref.refs_5_.wq_ref.wk_ref.wv_ref = bf16[1024,2688]{1,0:T(8,128)(2,1)} async-done(((bf16[64,2688]{1,0:T(8,128)(2,1)}), bf16[1024,2688]{1,0:T(8,128)(2,1)}) %all-gather.3.cloned.1.call-update) | async-done | bytes 5505040 | tf_op jit(solution)/shard_map/all_gather | solution.py:513
  74.4 1.0 slice.141
  76.2 2.7 fusion.5.x_ref
  79.7 9.8 %shard_map.299.q_ref.k_ref.v_ref = bf16[1024,1536]{1,0:T(8,128)(2,1)} custom-call(bf16[1024,1024]{1,0:T(8,128)(2,1)} %fusion.5.x_ref, bf16[1024,2688]{1,0:T(8,128)(2,1)} %all-gather.3.cloned.1.call-done.w_ref.refs_5_.wq_ref.wk_ref.wv_ref, f32[1,1536]{1,0:T(1,128)} %bitcast.142, f32[1024,128]{1,0:T(8,128)} %get-tuple-element.105.cos_ref, ...), custom_call_target="tpu_custom_call" | custom-call | flops 3221225472 | bytes 8388608 | tf_op jit(solution)/shard_map/pallas_call | solution.py:83
  89.5 15.8 %shard_map.300 = (bf16[1024,512]{1,0:T(8,128)(2,1)}, f32[1024,512]{1,0:T(8,128)}) custom-call(bf16[1024,1536]{1,0:T(8,128)(2,1)} %shard_map.299.q_ref.k_ref.v_ref, bf16[1024,1536]{1,0:T(8,128)(2,1)} %shard_map.299.q_ref.k_ref.v_ref, bf16[1024,1536]{1,0:T(8,128)(2,1)} %shard_map.299.q_ref.k_ref.v_ref), custom_call_target="tpu_custom_call" | custom-call | flops 8589934592 | bytes 6291456 | tf_op jit(solution)/shard_map/pallas_call | solution.py:193
  105.3 1.3 fusion.30
  106.6 1.5 collective-permute-start.3
  108.1 12.6 %collective-permute-done.3 = bf16[512,512]{1,0:T(8,128)(2,1)S(1)} collective-permute-done((bf16[512,512]{1,0:T(8,128)(2,1)S(1)}, bf16[512,512]{1,0:T(8,128)(2,1)S(1)}, u32[]{:S(2)}, u32[]{:S(2)}) %collective-permute-start.3) | collective-permute-done | bytes 524320 | tf_op jit(solution)/shard_map/ppermute | solution.py:560
  121.1 1.1 pad_maximum_fusion.1.att_ref
  122.2 4.9 %shard_map.301 = (f32[512,1024]{1,0:T(8,128)}, bf16[512,1024]{1,0:T(8,128)(2,1)}) custom-call(bf16[512,1024]{1,0:T(8,128)(2,1)} %pad_maximum_fusion.1.att_ref, bf16[1024,2688]{1,0:T(8,128)(2,1)} %all-gather.3.cloned.1.call-done.w_ref.refs_5_.wq_ref.wk_ref.wv_ref, bf16[512,1024]{1,0:T(8,128)(2,1)} %bitcast.105, f32[1,1024]{1,0:T(1,128)} %get-tuple-element.95.b_ref, ...), custom_call_target="tpu_custom_call" | custom-call | flops 1073741824 | bytes 7340032 | tf_op jit(solution)/shard_map/pallas_call | solution.py:256
  127.1 1.5 collective-permute-start.4
  129.4 20.6 %all-gather.5.cloned.1.call-done.up_ref.down_ref = bf16[1024,4096]{1,0:T(8,128)(2,1)} async-done(((bf16[64,4096]{1,0:T(8,128)(2,1)}), bf16[1024,4096]{1,0:T(8,128)(2,1)}) %all-gather.5.cloned.1.call-update) | async-done | bytes 8388624 | tf_op jit(solution)/shard_map/all_gather | solution.py:513
  150.1 17.0 %shard_map.302 = (bf16[512,2048]{1,0:T(8,128)(2,1)}, bf16[512,2048]{1,0:T(8,128)(2,1)}, f32[512,1024]{1,0:T(8,128)}, f32[512,1024]{1,0:T(8,128)}, f32[1,2048]{1,0:T(1,128)}) custom-call(bf16[512,1024]{1,0:T(8,128)(2,1)} %get-tuple-element.45.x_ref.refs_0_, bf16[512,1024]{1,0:T(8,128)(2,1)} %bitcast.125, ...), custom_call_target="tpu_custom_call" | custom-call | flops 8589934592 | bytes 16777216 | tf_op jit(solution)/shard_map/pallas_call | solution.py:400
  167.1 1.0 copy-done.21
  168.1 16.0 %shard_map.303 = (bf16[512,2048]{1,0:T(8,128)(2,1)}, bf16[512,2048]{1,0:T(8,128)(2,1)}, bf16[512,1024]{1,0:T(8,128)(2,1)}, bf16[512,1024]{1,0:T(8,128)(2,1)}, f32[1,2048]{1,0:T(1,128)}) custom-call(bf16[512,1024]{1,0:T(8,128)(2,1)} %copy-done.21, bf16[512,1024]{1,0:T(8,128)(2,1)} %collective-permute-done.1.og_ref.refs_7_, ...), custom_call_target="tpu_custom_call" | custom-call | flops 8589934592 | bytes 16777216 | tf_op jit(solution)/shard_map/pallas_call | solution.py:400
  184.0 15.6 %shard_map.304 = bf16[1024,4096]{1,0:T(8,128)(2,1)} custom-call(bf16[512,1024]{1,0:T(8,128)(2,1)} %get-tuple-element.45.x_ref.refs_0_, bf16[512,1024]{1,0:T(8,128)(2,1)} %copy-done.21, bf16[512,2048]{1,0:T(8,128)(2,1)} %get-tuple-element.50.refs_2_, bf16[512,2048]{1,0:T(8,128)(2,1)} %get-tuple-element.51.refs_3_, ...), custom_call_target="tpu_custom_call" | custom-call | flops 8589934592 | bytes 20971520 | tf_op jit(solution)/shard_map/pallas_call | solution.py:454
  199.8 1.1 copy-done.20
  200.9 1.5 collective-permute-start.6
  202.4 23.9 %collective-permute-done.6.refs_1_ = bf16[512,1024]{1,0:T(8,128)(2,1)S(1)} collective-permute-done((bf16[512,1024]{1,0:T(8,128)(2,1)S(1)}, bf16[512,1024]{1,0:T(8,128)(2,1)S(1)}, u32[]{:S(2)}, u32[]{:S(2)}) %collective-permute-start.6) | collective-permute-done | bytes 1048608 | tf_op jit(solution)/shard_map/ppermute | solution.py:567
  226.2 1.0 copy-done.5
  227.2 8.1 %shard_map.305 = (f32[512,1024]{1,0:T(8,128)}, bf16[512,1024]{1,0:T(8,128)(2,1)}, bf16[512,1024]{1,0:T(8,128)(2,1)}, f32[8,1024]{1,0:T(8,128)}) custom-call(f32[512,1024]{1,0:T(8,128)} %get-tuple-element.54.refs_0_, bf16[512,1024]{1,0:T(8,128)(2,1)} %copy-done.5, f32[512,1024]{1,0:T(8,128)} %get-tuple-element.44.refs_2_, bf16[512,1024]{1,0:T(8,128)(2,1)} %bitcast.127, ...), custom_call_target="tpu_custom_call" | custom-call | flops 1073741824 | bytes 11534336 | tf_op jit(solution)/shard_map/pallas_call | solution.py:289
  235.3 1.8 reshape.164
  237.2 2.2 constant_dynamic-slice_fusion.1
  239.5 1.2 collective-permute-start.7
  241.3 11.0 %collective-permute-done.7 = bf16[512,512]{1,0:T(8,128)(2,1)S(1)} collective-permute-done((bf16[512,512]{1,0:T(8,128)(2,1)S(1)}, bf16[512,512]{1,0:T(8,128)(2,1)S(1)}, u32[]{:S(2)}, u32[]{:S(2)}) %collective-permute-start.7) | collective-permute-done | bytes 524320 | tf_op jit(solution)/shard_map/ppermute | solution.py:577
  252.3 1.0 pad_maximum_fusion.2.do_ref
  253.3 30.5 %shard_map.306 = (bf16[1024,512]{1,0:T(8,128)(2,1)}, bf16[1024,512]{1,0:T(8,128)(2,1)}, bf16[1024,512]{1,0:T(8,128)(2,1)}) custom-call(bf16[1024,1536]{1,0:T(8,128)(2,1)} %shard_map.299.q_ref.k_ref.v_ref, bf16[1024,1536]{1,0:T(8,128)(2,1)} %shard_map.299.q_ref.k_ref.v_ref, bf16[1024,1536]{1,0:T(8,128)(2,1)} %shard_map.299.q_ref.k_ref.v_ref, ...), custom_call_target="tpu_custom_call" | custom-call | flops 21474836480 | bytes 10485760 | tf_op jit(solution)/shard_map/pallas_call | solution.py:208
  283.8 1.4 convert_reduce_fusion.3
  285.3 1.9 convert_reduce_fusion.1
  287.4 5.7 %shard_map.307 = (f32[512,1024]{1,0:T(8,128)}, f32[8,1024]{1,0:T(8,128)}) custom-call(bf16[1024,512]{1,0:T(8,128)(2,1)} %get-tuple-element.57.dq_ref, bf16[1024,512]{1,0:T(8,128)(2,1)} %get-tuple-element.58.dk_ref, bf16[1024,512]{1,0:T(8,128)(2,1)} %get-tuple-element.59.dv_ref, ...), custom_call_target="tpu_custom_call" | custom-call | flops 1610612736 | bytes 7864320 | tf_op jit(solution)/shard_map/pallas_call | solution.py:338
  293.2 5.4 %shard_map.308 = (bf16[512,1024]{1,0:T(8,128)(2,1)}, f32[8,1024]{1,0:T(8,128)}) custom-call(bf16[1024,512]{1,0:T(8,128)(2,1)} %get-tuple-element.57.dq_ref, bf16[1024,512]{1,0:T(8,128)(2,1)} %get-tuple-element.58.dk_ref, bf16[1024,512]{1,0:T(8,128)(2,1)} %get-tuple-element.59.dv_ref, ...), custom_call_target="tpu_custom_call" | custom-call | flops 1610612736 | bytes 7864320 | tf_op jit(solution)/shard_map/pallas_call | solution.py:338
  298.6 0.8 slice_add_fusion
  299.5 0.8 pad.9.small_ref
  300.4 9.4 %shard_map.310 = bf16[1024,2688]{1,0:T(8,128)(2,1)} custom-call(bf16[512,1024]{1,0:T(8,128)(2,1)} %pad_maximum_fusion.1.att_ref, bf16[512,1024]{1,0:T(8,128)(2,1)} %get-tuple-element.63.branch_ref, bf16[1024,1024]{1,0:T(8,128)(2,1)} %fusion.5.x_ref, bf16[1024,512]{1,0:T(8,128)(2,1)} %get-tuple-element.57.dq_ref, bf16[1024,512]{1,0:T(8,128)(2,1)} %get-tuple-element.58.dk_ref, ...), custom_call_target="tpu_custom_call" | custom-call | flops 4294967296 | bytes 10747904 | tf_op jit(solution)/shard_map/pallas_call | solution.py:482
  309.8 1.5 collective-permute-start.5
  312.0 1.5 collective-permute-start.10
  313.6 22.7 %collective-permute-done.5 = bf16[512,1024]{1,0:T(8,128)(2,1)S(1)} collective-permute-done((bf16[512,1024]{1,0:T(8,128)(2,1)}, bf16[512,1024]{1,0:T(8,128)(2,1)S(1)}, u32[]{:S(2)}, u32[]{:S(2)}) %collective-permute-start.5) | collective-permute-done | bytes 1048608 | tf_op jit(solution)/shard_map/ppermute | solution.py:568
  336.2 3.2 fusion.6
  339.4 19.3 %collective-permute-done.8.refs_1_ = bf16[512,1024]{1,0:T(8,128)(2,1)S(1)} collective-permute-done((bf16[512,1024]{1,0:T(8,128)(2,1)}, bf16[512,1024]{1,0:T(8,128)(2,1)S(1)}, u32[]{:S(2)}, u32[]{:S(2)}) %collective-permute-start.8) | collective-permute-done | bytes 1048608 | tf_op jit(solution)/shard_map/ppermute | solution.py:582
  358.7 1.0 copy-done.6
  359.7 4.5 %shard_map.309 = f32[512,1024]{1,0:T(8,128)} custom-call(f32[512,1024]{1,0:T(8,128)} %get-tuple-element.60.refs_0_, bf16[512,1024]{1,0:T(8,128)(2,1)} %copy-done.6, bf16[512,1024]{1,0:T(8,128)(2,1)} %bitcast.107, f32[512,1024]{1,0:T(8,128)} %get-tuple-element.62.refs_3_, f32[1,1024]{1,0:T(1,128)} %copy-done.10), custom_call_target="tpu_custom_call" | custom-call | flops 10485760 | bytes 7340032 | tf_op jit(solution)/shard_map/pallas_call | solution.py:312
  364.2 1.5 collective-permute-start.11
  366.0 22.5 %reduce-scatter.5.cloned.1.call-done = bf16[64,2688]{1,0:T(8,128)(2,1)} async-done(((bf16[1024,2688]{1,0:T(8,128)(2,1)}), bf16[64,2688]{1,0:T(8,128)(2,1)}) %reduce-scatter.5.cloned.1.call-update) | async-done | bytes 344080 | tf_op jit(solution)/shard_map/reduce_scatter | solution.py:516
  388.5 1.5 collective-permute-start.9
  390.1 0.8 copy.170
  390.9 1.8 reshape.178
  392.9 1.1 maximum_convert_fusion.1
  394.0 3.7 collective-permute-done.9
  398.0 0.8 slice_reduce_fusion
  398.9 0.7 slice.158
  400.8 1.6 reshape.177
  (124 shorter events, 9.7 us)
Async XLA Ops:
  7.2 7.0 %copy-start = (bf16[256,1024]{1,0:T(8,128)(2,1)S(1)}, bf16[256,1024]{1,0:T(8,128)(2,1)}, u32[]{:S(2)}) copy-start(bf16[256,1024]{1,0:T(8,128)(2,1)} %param.32) | copy-start | bytes 1572868
  7.2 7.0 %copy-start.7 = (bf16[64,4096]{1,0:T(8,128)(2,1)S(1)}, bf16[64,4096]{1,0:T(8,128)(2,1)}, u32[]{:S(2)}) copy-start(bf16[64,4096]{1,0:T(8,128)(2,1)} %param.30) | copy-start | bytes 1572868
  7.2 67.2 %all-gather.3.cloned.1.call-start = ((), (), s32[]{:S(2)}) async-start(), calls=%async_computation.2 | async-start | bytes 5849088 | tf_op jit(solution)/shard_map/all_gather | solution.py:513
  14.1 135.9 %all-gather.5.cloned.1.call-start = ((), (), s32[]{:S(2)}) async-start(), calls=%async_computation.3 | async-start | bytes 8912896 | tf_op jit(solution)/shard_map/all_gather | solution.py:513
  14.2 3.2 copy-start.2
  14.3 6.2 %copy-start.14 = (s32[3,1,512]{2,1,0:T(1,128)S(1)}, s32[3,1,512]{2,1,0:T(1,128)}, u32[]{:S(2)}) copy-start(s32[3,1,512]{2,1,0:T(1,128)} %param.21) | copy-start | bytes 18436
  14.3 30.3 %copy-start.15 = (f32[128]{0:T(128)S(1)}, f32[128]{0:T(128)}, u32[]{:S(2)}) copy-start(f32[128]{0:T(128)} %constant.110.clone) | copy-start | bytes 1540
  14.3 30.3 %copy-start.16 = (pred[128]{0:T(512)(128)(4,1)S(1)}, pred[128]{0:T(512)(128)(4,1)}, u32[]{:S(2)}) copy-start(pred[128]{0:T(512)(128)(4,1)} %constant.112.clone) | copy-start | bytes 388
  14.3 30.3 %copy-start.17 = (pred[128]{0:T(512)(128)(4,1)S(1)}, pred[128]{0:T(512)(128)(4,1)}, u32[]{:S(2)}) copy-start(pred[128]{0:T(512)(128)(4,1)} %constant.108.clone) | copy-start | bytes 388
  14.3 30.3 %copy-start.18 = (pred[128]{0:T(512)(128)(4,1)S(1)}, pred[128]{0:T(512)(128)(4,1)}, u32[]{:S(2)}) copy-start(pred[128]{0:T(512)(128)(4,1)} %constant.109.clone) | copy-start | bytes 388
  14.3 30.3 %copy-start.19 = (pred[128]{0:T(512)(128)(4,1)S(1)}, pred[128]{0:T(512)(128)(4,1)}, u32[]{:S(2)}) copy-start(pred[128]{0:T(512)(128)(4,1)} %constant.111.clone) | copy-start | bytes 388
  17.2 292.6 %reduce-scatter.3.cloned.1.call-start = ((), (), s32[]{:S(2)}) async-start(), calls=%async_computation.4 | async-start | bytes 8912896 | tf_op jit(solution)/shard_map/reduce_scatter | solution.py:516
  17.4 30.8 %collective-permute-start = (bf16[512,1024]{1,0:T(8,128)(2,1)S(1)}, bf16[512,1024]{1,0:T(8,128)(2,1)S(1)}, u32[]{:S(2)}, u32[]{:S(2)}) collective-permute-start(bf16[512,1024]{1,0:T(8,128)(2,1)S(1)} %bitcast.108), channel_id=1, source_target_pairs={{0,1},{1,0},{2,3},{3,2},{4,5},{5,4},{6,7},{7,6},{8,9},{9,8},{10,11... | collective-permute-start | bytes 3145736 | tf_op jit(solution)/shard_map/ppermute | solution.py:519
  20.5 24.1 %collective-permute-start.2 = (f32[3,512]{1,0:T(4,128)S(1)}, f32[3,512]{1,0:T(4,128)S(1)}, u32[]{:S(2)}, u32[]{:S(2)}) collective-permute-start(f32[3,512]{1,0:T(4,128)S(1)} %bitcast.139), channel_id=1, source_target_pairs={{0,1},{1,0},{2,3},{3,2},{4,5},{5,4},{6,7},{7,6},{8,9},{9,8},{10,11... | collective-permute-start | bytes 18440 | tf_op jit(solution)/shard_map/ppermute | solution.py:519
  20.6 58.4 %collective-permute-start.1 = (bf16[512,1024]{1,0:T(8,128)(2,1)}, bf16[512,1024]{1,0:T(8,128)(2,1)}, u32[]{:S(2)}, u32[]{:S(2)}) collective-permute-start(bf16[512,1024]{1,0:T(8,128)(2,1)} %bitcast.124), channel_id=1, source_target_pairs={{0,1},{1,0},{2,3},{3,2},{4,5},{5,4},{6,7},{7,6},{8,9},{9,8},{10,11... | collective-permute-start | bytes 3145736 | tf_op jit(solution)/shard_map/ppermute | solution.py:519
  48.2 27.9 %copy-start.3 = (bf16[512,1024]{1,0:T(8,128)(2,1)}, bf16[512,1024]{1,0:T(8,128)(2,1)S(1)}, u32[]{:S(2)}) copy-start(bf16[512,1024]{1,0:T(8,128)(2,1)S(1)} %collective-permute-done.tokens_ref) | copy-start | bytes 3145732
  76.2 2.7 copy-start.10
  106.6 14.1 %collective-permute-start.3 = (bf16[512,512]{1,0:T(8,128)(2,1)S(1)}, bf16[512,512]{1,0:T(8,128)(2,1)S(1)}, u32[]{:S(2)}, u32[]{:S(2)}) collective-permute-start(bf16[512,512]{1,0:T(8,128)(2,1)S(1)} %get-tuple-element.83), channel_id=1, source_target_pairs={{0,1},{1,0},{2,3},{3,2},{4,5},{5,4},{6,7},{7,6},{8,9},{9,8},{10,11... | collective-permute-start | bytes 1572872 | tf_op jit(solution)/shard_map/ppermute | solution.py:560
  127.1 39.9 %collective-permute-start.4 = (bf16[512,1024]{1,0:T(8,128)(2,1)}, bf16[512,1024]{1,0:T(8,128)(2,1)S(1)}, u32[]{:S(2)}, u32[]{:S(2)}) collective-permute-start(bf16[512,1024]{1,0:T(8,128)(2,1)} %get-tuple-element.45.x_ref.refs_0_), channel_id=1, source_target_pairs={{0,1},{1,0},{2,3},{3,2},{4,5},{5,4},{6,7},{7,6},{8,9},{9,8},{10,11... | collective-permute-start | bytes 3145736 | tf_op jit(solution)/shard_map/ppermute | solution.py:519
  167.1 1.0 copy-start.21
  199.7 1.2 copy-start.20
  199.7 188.8 %reduce-scatter.5.cloned.1.call-start = ((), (), s32[]{:S(2)}) async-start(), calls=%async_computation.5 | async-start | bytes 5849088 | tf_op jit(solution)/shard_map/reduce_scatter | solution.py:516
  200.9 25.3 %collective-permute-start.6 = (bf16[512,1024]{1,0:T(8,128)(2,1)S(1)}, bf16[512,1024]{1,0:T(8,128)(2,1)S(1)}, u32[]{:S(2)}, u32[]{:S(2)}) collective-permute-start(bf16[512,1024]{1,0:T(8,128)(2,1)S(1)} %copy-done.20), channel_id=1, source_target_pairs={{0,1},{1,0},{2,3},{3,2},{4,5},{5,4},{6,7},{7,6},{8,9},{9,8},{10,11... | collective-permute-start | bytes 3145736 | tf_op jit(solution)/shard_map/ppermute | solution.py:567
  226.2 1.0 copy-start.5
  237.1 3.7 copy-start.11
  237.1 3.6 copy-start.12
  239.3 1.9 copy-start.13
  239.5 12.8 %collective-permute-start.7 = (bf16[512,512]{1,0:T(8,128)(2,1)S(1)}, bf16[512,512]{1,0:T(8,128)(2,1)S(1)}, u32[]{:S(2)}, u32[]{:S(2)}) collective-permute-start(bf16[512,512]{1,0:T(8,128)(2,1)S(1)} %bitcast.129), channel_id=1, source_target_pairs={{0,1},{1,0},{2,3},{3,2},{4,5},{5,4},{6,7},{7,6},{8,9},{9,8},{10,11... | collective-permute-start | bytes 1572872 | tf_op jit(solution)/shard_map/ppermute | solution.py:577
  309.8 26.4 %copy-start.4 = (f32[512,1024]{1,0:T(8,128)S(1)}, f32[512,1024]{1,0:T(8,128)}, u32[]{:S(2)}) copy-start(f32[512,1024]{1,0:T(8,128)} %get-tuple-element.44.refs_2_) | copy-start | bytes 6291460
  309.8 2.1 copy-start.8
  309.8 26.4 %collective-permute-start.5 = (bf16[512,1024]{1,0:T(8,128)(2,1)}, bf16[512,1024]{1,0:T(8,128)(2,1)S(1)}, u32[]{:S(2)}, u32[]{:S(2)}) collective-permute-start(bf16[512,1024]{1,0:T(8,128)(2,1)} %get-tuple-element.47), channel_id=1, source_target_pairs={{0,1},{1,0},{2,3},{3,2},{4,5},{5,4},{6,7},{7,6},{8,9},{9,8},{10,11... | collective-permute-start | bytes 3145736 | tf_op jit(solution)/shard_map/ppermute | solution.py:568
  311.4 47.3 %collective-permute-start.8 = (bf16[512,1024]{1,0:T(8,128)(2,1)}, bf16[512,1024]{1,0:T(8,128)(2,1)S(1)}, u32[]{:S(2)}, u32[]{:S(2)}) collective-permute-start(bf16[512,1024]{1,0:T(8,128)(2,1)} %get-tuple-element.61), channel_id=1, source_target_pairs={{0,1},{1,0},{2,3},{3,2},{4,5},{5,4},{6,7},{7,6},{8,9},{9,8},{10,11... | collective-permute-start | bytes 3145736 | tf_op jit(solution)/shard_map/ppermute | solution.py:582
  312.0 53.7 %collective-permute-start.10 = (bf16[64,2048]{1,0:T(8,128)(2,1)S(1)}, bf16[64,2048]{1,0:T(8,128)(2,1)S(1)}, u32[]{:S(2)}, u32[]{:S(2)}) collective-permute-start(bf16[64,2048]{1,0:T(8,128)(2,1)S(1)} %get-tuple-element.89), channel_id=1, source_target_pairs={{0,1},{1,0},{2,3},{3,2},{4,5},{5,4},{6,7},{7,6},{8,9},{9,8},{10,11... | collective-permute-start | bytes 786440 | tf_op jit(solution)/shard_map/ppermute | solution.py:607
  358.7 1.0 copy-start.6
  364.2 28.6 %collective-permute-start.11 = (bf16[128,1024]{1,0:T(8,128)(2,1)S(1)}, bf16[128,1024]{1,0:T(8,128)(2,1)S(1)}, u32[]{:S(2)}, u32[]{:S(2)}) collective-permute-start(bf16[128,1024]{1,0:T(8,128)(2,1)S(1)} %bitcast.114), channel_id=1, source_target_pairs={{0,1},{1,0},{2,3},{3,2},{4,5},{5,4},{6,7},{7,6},{8,9},{9,8},{10,11... | collective-permute-start | bytes 786440 | tf_op jit(solution)/shard_map/ppermute | solution.py:607
  388.5 9.2 %collective-permute-start.9 = (bf16[64,2688]{1,0:T(8,128)(2,1)}, bf16[64,2688]{1,0:T(8,128)(2,1)S(1)}, u32[]{:S(2)}, u32[]{:S(2)}) collective-permute-start(bf16[64,2688]{1,0:T(8,128)(2,1)} %reduce-scatter.5.cloned.1.call-done), channel_id=1, source_target_pairs={{0,1},{1,0},{2,3},{3,2},{4,5},{5,4},{6,7},{7,6},{8,9},{9,8},{10,11... | collective-permute-start | bytes 1032200 | tf_op jit(solution)/shard_map/ppermute | solution.py:607
  390.9 6.8 %copy-start.9 = (bf16[64,2688]{1,0:T(8,128)(2,1)S(1)}, bf16[64,2688]{1,0:T(8,128)(2,1)}, u32[]{:S(2)}) copy-start(bf16[64,2688]{1,0:T(8,128)(2,1)} %reduce-scatter.5.cloned.1.call-done) | copy-start | bytes 1032196
  400.0 3.8 copy-start.1
Sparse Core Ops, SparseCore 0:
  14.2 60.0 all-gather.2
  76.5 73.4 all-gather.4
  199.8 102.8 reduce-scatter.2
  310.0 78.5 reduce-scatter.4
